TPU v7x, 128 devices: a whole 4x4x4 slice. The times are simulated.
128 devices in a mesh: dp: 2 (over z_hi), pipe: 8 (over z_lo, x), mp: 8 (over y, core).
Axes of the slice: x: 4, y: 4, z: 4 (z_hi: 2, z_lo: 2; z = z_hi * 2 + z_lo), core: 2. Of those that a mesh axis runs over, the one named last changes fastest.
Arguments:
- inputs: bfloat16 [4, 128, 1024], P(None, 'dp', 'mp'), may hold values from -6 to 6
- cotangent: bfloat16 [4, 128, 1024], P(None, 'dp', 'mp'), may hold values from -6 to 6
- gain: float32 [8, 1024], P('pipe'), may hold values from 0.25 to 1.75
- weight_in: bfloat16 [8, 1024, 32768], P('pipe', None, 'mp'), may hold values from -0.1875 to 0.1875
- weight_out: bfloat16 [8, 32768, 1024], P('pipe', 'mp'), may hold values from -0.03125 to 0.03125
Outputs:
- grad_in: bfloat16 [8, 1024, 32768], P('pipe', 'dp', 'mp')
- grad_out: bfloat16 [8, 32768, 1024], P('pipe', 'mp', 'dp')
- grad_gain: float32 [8, 1024], P('pipe', 'mp')
All inputs are finite; a program needn't handle non-finite values.
Results may differ from a plain program's by a relative error of at most 0.023.
Values may be sent and summed in bfloat16 or wider, within the bound.
No kernel may reach another device: no remote copies, remote signals or barrier semaphores. Data moves between devices by JAX's collectives and lax.ppermute only.
A program may use at most 128 MiB of HBM per device.

v0:
```python
import math

import jax
import jax.numpy as jnp
from jax import lax
from jax.sharding import PartitionSpec as P

GELU_COEF = math.sqrt(2.0 / math.pi)
CUBIC_COEF = 0.044715
NORM_EPS = 1e-06
CONTRACT_LAST = (((1,), (1,)), ((), ()))
CONTRACT_FIRST = (((0,), (0,)), ((), ()))


def shifted(shard, axis, by):
    count = lax.axis_size(axis)
    pairs = [(i, i + by) for i in range(count) if 0 <= i + by < count]
    return lax.ppermute(shard, axis, pairs)


def gelu_parts(values):
    tangent = jnp.tanh(GELU_COEF * (values + CUBIC_COEF * values * values * values))
    output = 0.5 * values * (1.0 + tangent)
    derivative = 0.5 * (1.0 + tangent) + 0.5 * values * (1.0 - tangent * tangent) * GELU_COEF * (
        1.0 + 3.0 * CUBIC_COEF * values * values
    )
    return (output, derivative)


def shards(inputs, cotangent, gain, weight_in, weight_out):
    segment_count = lax.axis_size("pipe")
    section = lax.axis_index("pipe")
    part_index = lax.axis_index("mp")
    micro, row_count, width = inputs.shape
    weight_first = weight_in[0]
    weight_second = weight_out[0]
    gain_row = gain[0]
    full_width = gain_row.shape[0]
    hidden = weight_first.shape[1]
    gain_own = lax.dynamic_slice_in_dim(gain_row, part_index * width, width, 0)
    turns = segment_count + micro - 1

    def forward_turn(turn, carry):
        incoming, rows_save, scale_save, gate_save = carry
        micro_slot = turn - section
        is_active = (micro_slot >= 0) & (micro_slot < micro)
        slot_index = jnp.clip(micro_slot, 0, micro - 1)
        first_rows = lax.dynamic_index_in_dim(inputs, slot_index, 0, keepdims=False)
        segment_input = jnp.where(section == 0, first_rows, incoming)
        whole_rows = lax.all_gather(segment_input, "mp", axis=1, tiled=True)

        def forward_active(operands):
            gathered, rows_keep, scale_keep, gate_keep = operands
            values = gathered.astype(jnp.float32)
            inv_rms = lax.rsqrt(jnp.mean(values * values, axis=1) + NORM_EPS)
            normed = (values * inv_rms[:, None] * gain_row).astype(jnp.bfloat16)
            gate_input = jnp.dot(normed, weight_first, preferred_element_type=jnp.float32)
            activated = gelu_parts(gate_input)[0].astype(jnp.bfloat16)
            branch = jnp.dot(activated, weight_second, preferred_element_type=jnp.float32)
            rows_keep = lax.dynamic_update_index_in_dim(rows_keep, gathered, slot_index, 0)
            scale_keep = lax.dynamic_update_index_in_dim(scale_keep, inv_rms, slot_index, 0)
            gate_keep = lax.dynamic_update_index_in_dim(gate_keep, gate_input, slot_index, 0)
            return (branch, rows_keep, scale_keep, gate_keep)

        def forward_resting(operands):
            gathered, rows_keep, scale_keep, gate_keep = operands
            return (
                jnp.zeros((row_count, full_width), jnp.float32),
                rows_keep,
                scale_keep,
                gate_keep,
            )

        branch, rows_save, scale_save, gate_save = lax.cond(
            is_active,
            forward_active,
            forward_resting,
            (whole_rows, rows_save, scale_save, gate_save),
        )
        branch_sum = lax.psum_scatter(branch, "mp", scatter_dimension=1, tiled=True)
        result = (segment_input.astype(jnp.float32) + branch_sum).astype(jnp.bfloat16)
        passed = shifted(result, "pipe", 1)
        return (passed, rows_save, scale_save, gate_save)

    forward_init = (
        jnp.zeros((row_count, width), jnp.bfloat16),
        jnp.zeros((micro, row_count, full_width), jnp.bfloat16),
        jnp.zeros((micro, row_count), jnp.float32),
        jnp.zeros((micro, row_count, hidden), jnp.float32),
    )
    forward_out = lax.fori_loop(0, turns, forward_turn, forward_init)
    rows_save = forward_out[1]
    scale_save = forward_out[2]
    gate_save = forward_out[3]

    def backward_turn(turn, carry):
        incoming, pregrad_save, outgrad_save, gain_acc = carry
        micro_slot = turn - (segment_count - 1 - section)
        is_active = (micro_slot >= 0) & (micro_slot < micro)
        slot_index = jnp.clip(micro_slot, 0, micro - 1)
        last_rows = lax.dynamic_index_in_dim(cotangent, slot_index, 0, keepdims=False).astype(
            jnp.float32
        )
        grad_rows = jnp.where(section == segment_count - 1, last_rows, incoming)
        whole_grad = lax.all_gather(grad_rows.astype(jnp.bfloat16), "mp", axis=1, tiled=True)

        def backward_active(operands):
            gathered, pregrad_keep, outgrad_keep = operands
            gate_input = lax.dynamic_index_in_dim(gate_save, slot_index, 0, keepdims=False)
            slopes = gelu_parts(gate_input)[1]
            inner_grad = lax.dot_general(
                gathered, weight_second, CONTRACT_LAST, preferred_element_type=jnp.float32
            )
            pre_grad = (inner_grad * slopes).astype(jnp.bfloat16)
            norm_part = lax.dot_general(
                pre_grad, weight_first, CONTRACT_LAST, preferred_element_type=jnp.float32
            )
            pregrad_keep = lax.dynamic_update_index_in_dim(pregrad_keep, pre_grad, slot_index, 0)
            outgrad_keep = lax.dynamic_update_index_in_dim(outgrad_keep, gathered, slot_index, 0)
            return (norm_part, pregrad_keep, outgrad_keep)

        def backward_resting(operands):
            gathered, pregrad_keep, outgrad_keep = operands
            return (jnp.zeros((row_count, full_width), jnp.float32), pregrad_keep, outgrad_keep)

        norm_part, pregrad_save, outgrad_save = lax.cond(
            is_active, backward_active, backward_resting, (whole_grad, pregrad_save, outgrad_save)
        )
        values = lax.dynamic_index_in_dim(rows_save, slot_index, 0, keepdims=False).astype(
            jnp.float32
        )
        inv_rms = lax.dynamic_index_in_dim(scale_save, slot_index, 0, keepdims=False)
        unit_full = values * inv_rms[:, None]
        unit_own = lax.dynamic_slice_in_dim(unit_full, part_index * width, width, 1)
        norm_grad = lax.psum_scatter(norm_part, "mp", scatter_dimension=1, tiled=True)
        scaled = norm_grad * gain_own
        row_dot = lax.psum(jnp.sum(scaled * unit_own, axis=1), "mp")
        previous = grad_rows + inv_rms[:, None] * (
            scaled - unit_own * row_dot[:, None] / full_width
        )
        gain_acc = gain_acc + jnp.where(is_active, jnp.sum(norm_grad * unit_own, axis=0), 0.0)
        passed = shifted(previous, "pipe", -1)
        return (passed, pregrad_save, outgrad_save, gain_acc)

    backward_init = (
        jnp.zeros((row_count, width), jnp.float32),
        jnp.zeros((micro, row_count, hidden), jnp.bfloat16),
        jnp.zeros((micro, row_count, full_width), jnp.bfloat16),
        jnp.zeros((width,), jnp.float32),
    )
    backward_out = lax.fori_loop(0, turns, backward_turn, backward_init)
    all_rows = micro * row_count
    pregrad_all = backward_out[1].reshape(all_rows, hidden)
    outgrad_all = backward_out[2].reshape(all_rows, full_width)
    gain_acc = backward_out[3]
    normed_all = (
        (rows_save.astype(jnp.float32) * scale_save[:, :, None] * gain_row)
        .astype(jnp.bfloat16)
        .reshape(all_rows, full_width)
    )
    activated_all = gelu_parts(gate_save)[0].astype(jnp.bfloat16).reshape(all_rows, hidden)
    in_term = lax.dot_general(
        normed_all, pregrad_all, CONTRACT_FIRST, preferred_element_type=jnp.float32
    )
    out_term = lax.dot_general(
        outgrad_all, activated_all, CONTRACT_FIRST, preferred_element_type=jnp.float32
    )
    grad_sums = lax.psum_scatter(
        jnp.stack((in_term, out_term), axis=1).astype(jnp.bfloat16),
        "dp",
        scatter_dimension=0,
        tiled=True,
    ).astype(jnp.float32)
    in_part = grad_sums[:, 0]
    out_part = grad_sums[:, 1]
    grad_first = in_part.astype(jnp.bfloat16)[None]
    grad_second = out_part.astype(jnp.bfloat16).T[None]
    gain_total = lax.psum(gain_acc, "dp")[None]
    return (grad_first, grad_second, gain_total)


def solution(mesh):
    in_specs = (
        P(None, "dp", "mp"),
        P(None, "dp", "mp"),
        P("pipe", None),
        P("pipe", None, "mp"),
        P("pipe", "mp", None),
    )
    out_specs = (P("pipe", "dp", "mp"), P("pipe", "mp", "dp"), P("pipe", "mp"))
    return jax.shard_map(shards, mesh=mesh, in_specs=in_specs, out_specs=out_specs, check_vma=False)
```

profile of v0, /device:TPU:1, one launch (start us, length us, event | category | flops | bytes accessed | tf_op | source)
XLA Modules:
  0.0 1693.8 jit_solution(12804930879796162620)
XLA Ops:
  11.3 635.0 %while.42 = (s32[]{:T(128)}, bf16[64,128]{1,0:T(8,128)(2,1)S(1)}, bf16[4,64,1024]{2,1,0:T(8,128)(2,1)S(1)}, f32[4,64]{1,0:T(4,128)S(1)}, f32[4,64,4096]{2,1,0:T(...) while((s32[]{:T(128)}, bf16[64,128]{1,0:T(8,128)(2,1)S(1)}, ...), condition=%wide.region_5.6_spmd, body=%wide.region_0.5_spmd.sunk | while | flops 1076592640 | bytes 48142608 | solution.py:91
  34.2 26.1 %reduce-scatter.6.cloned.1.call-done = f32[64,128]{1,0:T(8,128)} async-done(((f32[64,1024]{1,0:T(8,128)}), f32[64,128]{1,0:T(8,128)}) %reduce-scatter.6.cloned.1.call-update) | async-done | bytes 32784 | tf_op jit(solution)/shard_map/while/body/eval_jaxpr/reduce_scatter | solution.py:80
  89.8 27.5 %reduce-scatter.6.cloned.1.call-done = f32[64,128]{1,0:T(8,128)} async-done(((f32[64,1024]{1,0:T(8,128)}), f32[64,128]{1,0:T(8,128)}) %reduce-scatter.6.cloned.1.call-update) | async-done | bytes 32784 | tf_op jit(solution)/shard_map/while/body/eval_jaxpr/reduce_scatter | solution.py:80
  146.7 28.9 %reduce-scatter.6.cloned.1.call-done = f32[64,128]{1,0:T(8,128)} async-done(((f32[64,1024]{1,0:T(8,128)}), f32[64,128]{1,0:T(8,128)}) %reduce-scatter.6.cloned.1.call-update) | async-done | bytes 32784 | tf_op jit(solution)/shard_map/while/body/eval_jaxpr/reduce_scatter | solution.py:80
  205.1 29.0 %reduce-scatter.6.cloned.1.call-done = f32[64,128]{1,0:T(8,128)} async-done(((f32[64,1024]{1,0:T(8,128)}), f32[64,128]{1,0:T(8,128)}) %reduce-scatter.6.cloned.1.call-update) | async-done | bytes 32784 | tf_op jit(solution)/shard_map/while/body/eval_jaxpr/reduce_scatter | solution.py:80
  255.6 36.9 %reduce-scatter.6.cloned.1.call-done = f32[64,128]{1,0:T(8,128)} async-done(((f32[64,1024]{1,0:T(8,128)}), f32[64,128]{1,0:T(8,128)}) %reduce-scatter.6.cloned.1.call-update) | async-done | bytes 32784 | tf_op jit(solution)/shard_map/while/body/eval_jaxpr/reduce_scatter | solution.py:80
  314.0 36.9 %reduce-scatter.6.cloned.1.call-done = f32[64,128]{1,0:T(8,128)} async-done(((f32[64,1024]{1,0:T(8,128)}), f32[64,128]{1,0:T(8,128)}) %reduce-scatter.6.cloned.1.call-update) | async-done | bytes 32784 | tf_op jit(solution)/shard_map/while/body/eval_jaxpr/reduce_scatter | solution.py:80
  372.4 36.7 %reduce-scatter.6.cloned.1.call-done = f32[64,128]{1,0:T(8,128)} async-done(((f32[64,1024]{1,0:T(8,128)}), f32[64,128]{1,0:T(8,128)}) %reduce-scatter.6.cloned.1.call-update) | async-done | bytes 32784 | tf_op jit(solution)/shard_map/while/body/eval_jaxpr/reduce_scatter | solution.py:80
  430.6 36.6 %reduce-scatter.6.cloned.1.call-done = f32[64,128]{1,0:T(8,128)} async-done(((f32[64,1024]{1,0:T(8,128)}), f32[64,128]{1,0:T(8,128)}) %reduce-scatter.6.cloned.1.call-update) | async-done | bytes 32784 | tf_op jit(solution)/shard_map/while/body/eval_jaxpr/reduce_scatter | solution.py:80
  488.8 36.7 %reduce-scatter.6.cloned.1.call-done = f32[64,128]{1,0:T(8,128)} async-done(((f32[64,1024]{1,0:T(8,128)}), f32[64,128]{1,0:T(8,128)}) %reduce-scatter.6.cloned.1.call-update) | async-done | bytes 32784 | tf_op jit(solution)/shard_map/while/body/eval_jaxpr/reduce_scatter | solution.py:80
  547.0 36.6 %reduce-scatter.6.cloned.1.call-done = f32[64,128]{1,0:T(8,128)} async-done(((f32[64,1024]{1,0:T(8,128)}), f32[64,128]{1,0:T(8,128)}) %reduce-scatter.6.cloned.1.call-update) | async-done | bytes 32784 | tf_op jit(solution)/shard_map/while/body/eval_jaxpr/reduce_scatter | solution.py:80
  605.1 36.4 %reduce-scatter.6.cloned.1.call-done = f32[64,128]{1,0:T(8,128)} async-done(((f32[64,1024]{1,0:T(8,128)}), f32[64,128]{1,0:T(8,128)}) %reduce-scatter.6.cloned.1.call-update) | async-done | bytes 32784 | tf_op jit(solution)/shard_map/while/body/eval_jaxpr/reduce_scatter | solution.py:80
  648.0 816.4 %while.43 = (s32[]{:T(128)}, f32[64,128]{1,0:T(8,128)S(1)}, bf16[4,64,4096]{2,1,0:T(8,128)(2,1)}, bf16[4,64,1024]{2,1,0:T(8,128)(2,1)S(1)}, f32[128]{0:T(128)S(1...) while((s32[]{:T(128)}, f32[64,128]{1,0:T(8,128)S(1)}, ...), condition=%wide.region_13.14_spmd.clone, body=%wide.region_6.13_spmd.clone.sunk | while | flops 1078878336 | bytes 56333856 | solution.py:151
  664.1 38.3 %reduce-scatter.8.cloned.1.call-done = f32[64,128]{1,0:T(8,128)} async-done(((f32[64,1024]{1,0:T(8,128)}), f32[64,128]{1,0:T(8,128)}) %reduce-scatter.8.cloned.1.call-update) | async-done | bytes 32784 | tf_op jit(solution)/shard_map/while/body/eval_jaxpr/reduce_scatter | solution.py:135
  738.0 37.9 %reduce-scatter.8.cloned.1.call-done = f32[64,128]{1,0:T(8,128)} async-done(((f32[64,1024]{1,0:T(8,128)}), f32[64,128]{1,0:T(8,128)}) %reduce-scatter.8.cloned.1.call-update) | async-done | bytes 32784 | tf_op jit(solution)/shard_map/while/body/eval_jaxpr/reduce_scatter | solution.py:135
  811.6 37.9 %reduce-scatter.8.cloned.1.call-done = f32[64,128]{1,0:T(8,128)} async-done(((f32[64,1024]{1,0:T(8,128)}), f32[64,128]{1,0:T(8,128)}) %reduce-scatter.8.cloned.1.call-update) | async-done | bytes 32784 | tf_op jit(solution)/shard_map/while/body/eval_jaxpr/reduce_scatter | solution.py:135
  885.1 37.9 %reduce-scatter.8.cloned.1.call-done = f32[64,128]{1,0:T(8,128)} async-done(((f32[64,1024]{1,0:T(8,128)}), f32[64,128]{1,0:T(8,128)}) %reduce-scatter.8.cloned.1.call-update) | async-done | bytes 32784 | tf_op jit(solution)/shard_map/while/body/eval_jaxpr/reduce_scatter | solution.py:135
  958.7 40.0 %reduce-scatter.8.cloned.1.call-done = f32[64,128]{1,0:T(8,128)} async-done(((f32[64,1024]{1,0:T(8,128)}), f32[64,128]{1,0:T(8,128)}) %reduce-scatter.8.cloned.1.call-update) | async-done | bytes 32784 | tf_op jit(solution)/shard_map/while/body/eval_jaxpr/reduce_scatter | solution.py:135
  1034.3 40.0 %reduce-scatter.8.cloned.1.call-done = f32[64,128]{1,0:T(8,128)} async-done(((f32[64,1024]{1,0:T(8,128)}), f32[64,128]{1,0:T(8,128)}) %reduce-scatter.8.cloned.1.call-update) | async-done | bytes 32784 | tf_op jit(solution)/shard_map/while/body/eval_jaxpr/reduce_scatter | solution.py:135
  1109.9 40.0 %reduce-scatter.8.cloned.1.call-done = f32[64,128]{1,0:T(8,128)} async-done(((f32[64,1024]{1,0:T(8,128)}), f32[64,128]{1,0:T(8,128)}) %reduce-scatter.8.cloned.1.call-update) | async-done | bytes 32784 | tf_op jit(solution)/shard_map/while/body/eval_jaxpr/reduce_scatter | solution.py:135
  1195.4 30.0 %reduce-scatter.8.cloned.1.call-done = f32[64,128]{1,0:T(8,128)} async-done(((f32[64,1024]{1,0:T(8,128)}), f32[64,128]{1,0:T(8,128)}) %reduce-scatter.8.cloned.1.call-update) | async-done | bytes 32784 | tf_op jit(solution)/shard_map/while/body/eval_jaxpr/reduce_scatter | solution.py:135
  1271.0 28.2 %reduce-scatter.8.cloned.1.call-done = f32[64,128]{1,0:T(8,128)} async-done(((f32[64,1024]{1,0:T(8,128)}), f32[64,128]{1,0:T(8,128)}) %reduce-scatter.8.cloned.1.call-update) | async-done | bytes 32784 | tf_op jit(solution)/shard_map/while/body/eval_jaxpr/reduce_scatter | solution.py:135
  1344.7 26.7 %reduce-scatter.8.cloned.1.call-done = f32[64,128]{1,0:T(8,128)} async-done(((f32[64,1024]{1,0:T(8,128)}), f32[64,128]{1,0:T(8,128)}) %reduce-scatter.8.cloned.1.call-update) | async-done | bytes 32784 | tf_op jit(solution)/shard_map/while/body/eval_jaxpr/reduce_scatter | solution.py:135
  1484.4 189.5 %reduce-scatter.4.cloned.1.call-done = bf16[512,2,4096]{2,0,1:T(8,128)(2,1)} async-done(((bf16[1024,2,4096]{2,0,1:T(8,128)(2,1)}), bf16[512,2,4096]{2,0,1:T(8,128)(2,1)}) %reduce-scatter.4.cloned.1.call-update) | async-done | bytes 8388624 | tf_op jit(solution)/shard_map/reduce_scatter | solution.py:168
  (377 shorter events, 834.0 us)
Async XLA Ops:
  11.3 49.0 %reduce-scatter.6.cloned.1.call-start = ((), (), s32[]{:S(2)}) async-start(), calls=%async_computation.4 | async-start | bytes 294912 | tf_op jit(solution)/shard_map/while/body/eval_jaxpr/reduce_scatter | solution.py:80
  65.1 52.1 %reduce-scatter.6.cloned.1.call-start = ((), (), s32[]{:S(2)}) async-start(), calls=%async_computation.4 | async-start | bytes 294912 | tf_op jit(solution)/shard_map/while/body/eval_jaxpr/reduce_scatter | solution.py:80
  122.0 53.6 %reduce-scatter.6.cloned.1.call-start = ((), (), s32[]{:S(2)}) async-start(), calls=%async_computation.4 | async-start | bytes 294912 | tf_op jit(solution)/shard_map/while/body/eval_jaxpr/reduce_scatter | solution.py:80
  180.4 53.6 %reduce-scatter.6.cloned.1.call-start = ((), (), s32[]{:S(2)}) async-start(), calls=%async_computation.4 | async-start | bytes 294912 | tf_op jit(solution)/shard_map/while/body/eval_jaxpr/reduce_scatter | solution.py:80
  238.9 53.6 %reduce-scatter.6.cloned.1.call-start = ((), (), s32[]{:S(2)}) async-start(), calls=%async_computation.4 | async-start | bytes 294912 | tf_op jit(solution)/shard_map/while/body/eval_jaxpr/reduce_scatter | solution.py:80
  297.3 53.6 %reduce-scatter.6.cloned.1.call-start = ((), (), s32[]{:S(2)}) async-start(), calls=%async_computation.4 | async-start | bytes 294912 | tf_op jit(solution)/shard_map/while/body/eval_jaxpr/reduce_scatter | solution.py:80
  355.6 53.4 %reduce-scatter.6.cloned.1.call-start = ((), (), s32[]{:S(2)}) async-start(), calls=%async_computation.4 | async-start | bytes 294912 | tf_op jit(solution)/shard_map/while/body/eval_jaxpr/reduce_scatter | solution.py:80
  413.9 53.4 %reduce-scatter.6.cloned.1.call-start = ((), (), s32[]{:S(2)}) async-start(), calls=%async_computation.4 | async-start | bytes 294912 | tf_op jit(solution)/shard_map/while/body/eval_jaxpr/reduce_scatter | solution.py:80
  472.0 53.4 %reduce-scatter.6.cloned.1.call-start = ((), (), s32[]{:S(2)}) async-start(), calls=%async_computation.4 | async-start | bytes 294912 | tf_op jit(solution)/shard_map/while/body/eval_jaxpr/reduce_scatter | solution.py:80
  530.2 53.4 %reduce-scatter.6.cloned.1.call-start = ((), (), s32[]{:S(2)}) async-start(), calls=%async_computation.4 | async-start | bytes 294912 | tf_op jit(solution)/shard_map/while/body/eval_jaxpr/reduce_scatter | solution.py:80
  588.4 53.1 %reduce-scatter.6.cloned.1.call-start = ((), (), s32[]{:S(2)}) async-start(), calls=%async_computation.4 | async-start | bytes 294912 | tf_op jit(solution)/shard_map/while/body/eval_jaxpr/reduce_scatter | solution.py:80
  648.0 54.4 %reduce-scatter.8.cloned.1.call-start = ((), (), s32[]{:S(2)}) async-start(), calls=%async_computation.5 | async-start | bytes 294912 | tf_op jit(solution)/shard_map/while/body/eval_jaxpr/reduce_scatter | solution.py:135
  723.9 52.0 %reduce-scatter.8.cloned.1.call-start = ((), (), s32[]{:S(2)}) async-start(), calls=%async_computation.5 | async-start | bytes 294912 | tf_op jit(solution)/shard_map/while/body/eval_jaxpr/reduce_scatter | solution.py:135
  792.9 4.7 collective-permute-start.1
  797.5 52.0 %reduce-scatter.8.cloned.1.call-start = ((), (), s32[]{:S(2)}) async-start(), calls=%async_computation.5 | async-start | bytes 294912 | tf_op jit(solution)/shard_map/while/body/eval_jaxpr/reduce_scatter | solution.py:135
  871.1 52.0 %reduce-scatter.8.cloned.1.call-start = ((), (), s32[]{:S(2)}) async-start(), calls=%async_computation.5 | async-start | bytes 294912 | tf_op jit(solution)/shard_map/while/body/eval_jaxpr/reduce_scatter | solution.py:135
  944.7 54.0 %reduce-scatter.8.cloned.1.call-start = ((), (), s32[]{:S(2)}) async-start(), calls=%async_computation.5 | async-start | bytes 294912 | tf_op jit(solution)/shard_map/while/body/eval_jaxpr/reduce_scatter | solution.py:135
  1020.2 54.0 %reduce-scatter.8.cloned.1.call-start = ((), (), s32[]{:S(2)}) async-start(), calls=%async_computation.5 | async-start | bytes 294912 | tf_op jit(solution)/shard_map/while/body/eval_jaxpr/reduce_scatter | solution.py:135
  1095.8 54.0 %reduce-scatter.8.cloned.1.call-start = ((), (), s32[]{:S(2)}) async-start(), calls=%async_computation.5 | async-start | bytes 294912 | tf_op jit(solution)/shard_map/while/body/eval_jaxpr/reduce_scatter | solution.py:135
  1171.4 54.0 %reduce-scatter.8.cloned.1.call-start = ((), (), s32[]{:S(2)}) async-start(), calls=%async_computation.5 | async-start | bytes 294912 | tf_op jit(solution)/shard_map/while/body/eval_jaxpr/reduce_scatter | solution.py:135
  1247.0 52.1 %reduce-scatter.8.cloned.1.call-start = ((), (), s32[]{:S(2)}) async-start(), calls=%async_computation.5 | async-start | bytes 294912 | tf_op jit(solution)/shard_map/while/body/eval_jaxpr/reduce_scatter | solution.py:135
  1320.8 50.7 %reduce-scatter.8.cloned.1.call-start = ((), (), s32[]{:S(2)}) async-start(), calls=%async_computation.5 | async-start | bytes 294912 | tf_op jit(solution)/shard_map/while/body/eval_jaxpr/reduce_scatter | solution.py:135
  1393.0 49.8 %reduce-scatter.8.cloned.1.call-start = ((), (), s32[]{:S(2)}) async-start(), calls=%async_computation.5 | async-start | bytes 294912 | tf_op jit(solution)/shard_map/while/body/eval_jaxpr/reduce_scatter | solution.py:135
  1464.4 209.5 %reduce-scatter.4.cloned.1.call-start = ((), (), s32[]{:S(2)}) async-start(), calls=%async_computation.3 | async-start | bytes 25165824 | tf_op jit(solution)/shard_map/reduce_scatter | solution.py:168
  (58 other events, 829.9 us)
Sparse Core Ops, SparseCore 0:
  34.3 25.9 reduce-scatter.5
  89.9 27.2 reduce-scatter.5
  146.8 28.7 reduce-scatter.5
  205.2 28.8 reduce-scatter.5
  255.7 36.7 reduce-scatter.5
  314.1 36.7 reduce-scatter.5
  372.5 36.5 reduce-scatter.5
  430.7 36.4 reduce-scatter.5
  488.9 36.5 reduce-scatter.5
  547.1 36.4 reduce-scatter.5
  605.3 36.2 reduce-scatter.5
  664.1 38.2 reduce-scatter.7
  738.1 37.7 reduce-scatter.7
  811.6 37.8 reduce-scatter.7
  885.2 37.7 reduce-scatter.7
  958.8 39.8 reduce-scatter.7
  1034.4 39.8 reduce-scatter.7
  1110.0 39.8 reduce-scatter.7
  1195.5 29.8 reduce-scatter.7
  1271.1 28.0 reduce-scatter.7
  1344.8 26.5 reduce-scatter.7
  1417.1 25.6 reduce-scatter.7
Sparse Core Ops, SparseCore 1:
  1478.7 195.2 reduce-scatter.3
where the time goes:
time: 1700 us; the launch traced here: 1690 us
  waiting for transfers between devices  987 us (58%)
  blocking collectives  485 us (29%)
  matrix products  77.9 us (5%)
  starting transfers between devices  49.2 us (3%)
  other arithmetic  43.7 us (3%)
  local copies, waits for them, and re-layouts  33.6 us (2%)
    reduce_scatter x11, waiting for transfers between devices, backward_turn(): lax.psum_scatter(norm_part, 'mp', scatter_dimension=1, tiled=True)  383 us
    reduce_scatter x11, waiting for transfers between devices, forward_turn(): branch_sum = lax.psum_scatter(branch, 'mp', scatter_dimension=1, tiled=True)  368 us
    reduce_scatter x1, waiting for transfers between devices, shards(): lax.psum_scatter(jnp.stack((in_term, out_term), axis=1).astype(jnp.bfloat...  190 us
    psum x11, blocking collectives, backward_turn(): row_dot = lax.psum(jnp.sum(scaled * unit_own, axis=1), 'mp')  166 us
    all_gather x11, blocking collectives, forward_turn(): whole_rows = lax.all_gather(segment_input, 'mp', axis=1, tiled=True)  166 us
    all_gather x11, blocking collectives, backward_turn(): lax.all_gather(grad_rows.astype(jnp.bfloat16), 'mp', axis=1, tiled=True)  147 us
    ppermute x22, starting transfers between devices, shifted(): return lax.ppermute(shard, axis, pairs)  49.2 us
    ppermute x22, waiting for transfers between devices, shifted(): return lax.ppermute(shard, axis, pairs)  46.1 us
  transfers between devices with their start and end apart: 45, of which 45 were waited for; matrix products, arithmetic and copies ran while one was open for 0% of the time, Pallas kernels for 0%

commit v1 on v0

v1 whole, which is shorter than its diff:
```python
import functools
import math

import jax
import jax.numpy as jnp
from jax import lax
from jax.experimental import pallas as pl
from jax.experimental.pallas import tpu as pltpu
from jax.sharding import PartitionSpec as P

GELU_COEF = math.sqrt(2.0 / math.pi)
CUBIC_COEF = 0.044715
NORM_EPS = 1e-06
BF16 = jnp.bfloat16
F32 = jnp.float32
NT = (((1,), (1,)), ((), ()))
TN = (((0,), (0,)), ((), ()))
MIB = 2**20
TILE = 512
VMEM = pltpu.VMEM
IN_VMEM = pl.BlockSpec(memory_space=pltpu.VMEM)
IN_SMEM = pl.BlockSpec(memory_space=pltpu.SMEM)
ANYWHERE = pl.BlockSpec(memory_space=pl.ANY)
IN_HBM = pl.BlockSpec(memory_space=pltpu.HBM)


def params(mib):
    return pltpu.CompilerParams(vmem_limit_bytes=int(mib * MIB))


def gelu_both(a):
    a2 = a * a
    t = jnp.tanh(a * (GELU_COEF + (GELU_COEF * CUBIC_COEF) * a2))
    h = 0.5 + 0.5 * t
    z = a * h
    slope = h + (a * (0.5 - 0.5 * t * t)) * (GELU_COEF + (3.0 * GELU_COEF * CUBIC_COEF) * a2)
    return z, slope


def load_body(wi, wo, wi_out, wo_out, sems):
    first = pltpu.make_async_copy(wi, wi_out, sems.at[0])
    second = pltpu.make_async_copy(wo, wo_out, sems.at[1])
    first.start()
    second.start()
    first.wait()
    second.wait()


def load_weights(wi, wo):
    return pl.pallas_call(
        load_body,
        out_shape=(VMEM(wi.shape, wi.dtype), VMEM(wo.shape, wo.dtype)),
        in_specs=[IN_HBM] * 2,
        out_specs=[IN_VMEM] * 2,
        scratch_shapes=[pltpu.SemaphoreType.DMA((2,))],
        compiler_params=params(1),
        name="load_weights",
    )(wi, wo)


def alloc_body(*refs):
    refs[-1][...] = jnp.zeros_like(refs[-1])


def alloc(shapes, dtypes):
    return pl.pallas_call(
        alloc_body,
        out_shape=tuple(VMEM(s, d) for s, d in zip(shapes, dtypes)),
        out_specs=[IN_VMEM] * len(shapes),
        compiler_params=params(1),
        name="alloc",
    )()


def norm_body(t, flags, a0, a1, a2, a3, gain, n_in, r_in, u_out, n_save, r_save):
    rows = a0.shape[0]

    @pl.when(flags[t] > 0)
    def _():
        for d, piece in enumerate((a0, a1, a2, a3)):
            x = piece[...].astype(F32)
            r = lax.rsqrt(jnp.mean(x * x, axis=1, keepdims=True) + NORM_EPS)
            n = x * r
            u_out[d * rows : (d + 1) * rows, :] = (n * gain[...]).astype(BF16)
            if d == 0:
                n_save[...] = n
                r_save[...] = jnp.broadcast_to(r, r_save.shape)


def norm_call(t, flags, pieces, gain, n_save, r_save):
    rows, width = pieces[0].shape
    return pl.pallas_call(
        functools.partial(norm_body, t),
        out_shape=(
            jax.ShapeDtypeStruct((4 * rows, width), BF16),
            VMEM(n_save.shape, F32),
            VMEM(r_save.shape, F32),
        ),
        in_specs=[IN_SMEM] + [IN_VMEM] * 7,
        out_specs=[IN_VMEM] * 3,
        input_output_aliases={6: 1, 7: 2},
        compiler_params=params(4),
        name=f"norm_t{t}",
    )(flags, *pieces, gain, n_save, r_save)


def forward_body(t, last, flags, u_own, u_oth, wi, wo, z_in, s_in, us_in, p_own, p_oth, z, s, us, acc, sems):
    half = u_own.shape[0]
    first = pltpu.make_async_copy(u_own, us.at[pl.ds(0, half)], sems.at[0])
    second = pltpu.make_async_copy(u_oth, us.at[pl.ds(half, half)], sems.at[1])

    @pl.when(flags[t] > 0)
    def _():
        first.start()
        second.start()
        u = jnp.concatenate([u_own[...], u_oth[...]], axis=0)
        for j in range(wi.shape[1] // TILE):
            cols = slice(j * TILE, (j + 1) * TILE)
            a = jnp.dot(u, wi[:, cols], preferred_element_type=F32)
            zf, slope = gelu_both(a)
            zb = zf.astype(BF16)
            z[:, cols] = zb
            s[:, cols] = slope.astype(BF16)
            if not last:
                d = jnp.dot(zb, wo[cols, :], preferred_element_type=F32)
                if j == 0:
                    acc[...] = d
                else:
                    acc[...] += d
        if not last:
            p_own[...] = acc[:half]
            p_oth[...] = acc[half:].astype(BF16)
        first.wait()
        second.wait()


def forward_call(t, last, flags, u_own, u_oth, wi, wo, z, s, us):
    shape = u_own.shape
    return pl.pallas_call(
        functools.partial(forward_body, t, last),
        out_shape=(
            VMEM(shape, F32),
            jax.ShapeDtypeStruct(shape, BF16),
            VMEM(z.shape, BF16),
            VMEM(s.shape, BF16),
            jax.ShapeDtypeStruct(us.shape, BF16),
        ),
        in_specs=[IN_SMEM] + [IN_VMEM] * 6 + [IN_HBM],
        out_specs=[IN_VMEM] * 4 + [IN_HBM],
        scratch_shapes=[VMEM((2 * shape[0], shape[1]), F32), pltpu.SemaphoreType.DMA((2,))],
        input_output_aliases={5: 2, 6: 3, 7: 4},
        compiler_params=params(14),
        name=f"forward_t{t}",
    )(flags, u_own, u_oth, wi, wo, z, s, us)


def backward_body(t, flags, e_own, e_oth, wi, wo, s, p_in, es_in, q_own, q_oth, p, es, acc, sems):
    half = e_own.shape[0]
    first = pltpu.make_async_copy(e_own, es.at[pl.ds(0, half)], sems.at[0])
    second = pltpu.make_async_copy(e_oth, es.at[pl.ds(half, half)], sems.at[1])

    @pl.when(flags[t] > 0)
    def _():
        first.start()
        second.start()
        e = jnp.concatenate([e_own[...], e_oth[...]], axis=0)
        for j in range(wi.shape[1] // TILE):
            cols = slice(j * TILE, (j + 1) * TILE)
            dz = lax.dot_general(e, wo[cols, :], NT, preferred_element_type=F32)
            pb = (dz * s[:, cols].astype(F32)).astype(BF16)
            p[:, cols] = pb
            d = lax.dot_general(pb, wi[:, cols], NT, preferred_element_type=F32)
            if j == 0:
                acc[...] = d
            else:
                acc[...] += d
        q_own[...] = acc[:half]
        q_oth[...] = acc[half:].astype(BF16)
        first.wait()
        second.wait()


def backward_call(t, flags, e_own, e_oth, wi, wo, s, p, es):
    shape = e_own.shape
    return pl.pallas_call(
        functools.partial(backward_body, t),
        out_shape=(
            VMEM(shape, F32),
            jax.ShapeDtypeStruct(shape, BF16),
            VMEM(p.shape, BF16),
            jax.ShapeDtypeStruct(es.shape, BF16),
        ),
        in_specs=[IN_SMEM] + [IN_VMEM] * 6 + [IN_HBM],
        out_specs=[IN_VMEM] * 3 + [IN_HBM],
        scratch_shapes=[VMEM((2 * shape[0], shape[1]), F32), pltpu.SemaphoreType.DMA((2,))],
        input_output_aliases={6: 2, 7: 3},
        compiler_params=params(14),
        name=f"backward_t{t}",
    )(flags, e_own, e_oth, wi, wo, s, p, es)


def norm_back_body(t, flags, q0, q1, q2, q3, g, gain, n_save, r_save, gg_in, out, gg):
    width = q0.shape[1]

    @pl.when(flags[t] > 0)
    def _():
        q = (q0[...] + q1[...].astype(F32)) + (q2[...].astype(F32) + q3[...].astype(F32))
        n = n_save[...]
        r = r_save[:, 0:1]
        qn = q * n
        gg[0:1, :] = jnp.sum(qn, axis=0, keepdims=True)
        dot = jnp.sum(qn * gain[...], axis=1, keepdims=True) / width
        back = r * (q * gain[...] - n * dot)
        out[...] = (back + g[...].astype(F32)).astype(BF16)


def norm_back_call(t, flags, terms, g, gain, n_save, r_save, gg):
    return pl.pallas_call(
        functools.partial(norm_back_body, t),
        out_shape=(jax.ShapeDtypeStruct(g.shape, BF16), VMEM(gg.shape, F32)),
        in_specs=[IN_SMEM] + [IN_VMEM] * 9,
        out_specs=[IN_VMEM] * 2,
        input_output_aliases={9: 1},
        compiler_params=params(4),
        name=f"norm_back_t{t}",
    )(flags, *terms, g, gain, n_save, r_save, gg)


def grads_body(side, us, u_peer, es, e_peer, wi, wo, z, p, gin, gout):
    at = pl.multiple_of(pl.program_id(0) * TILE, TILE)
    cols = pl.ds(at, TILE)
    half = gin.shape[0]
    mine = pl.ds(pl.multiple_of(side[0] * half, half), half)
    a = jnp.dot(u_peer[...], wi[:, cols], preferred_element_type=F32)
    zf, slope = gelu_both(a)
    dz = lax.dot_general(e_peer[...], wo[cols, :], NT, preferred_element_type=F32)
    gi = lax.dot_general(us[:, mine], p[:, cols], TN, preferred_element_type=F32)
    gi += lax.dot_general(
        u_peer[:, mine], (dz * slope).astype(BF16), TN, preferred_element_type=F32
    )
    gin[...] = gi.astype(BF16)
    go = lax.dot_general(z[:, cols], es[:, mine], TN, preferred_element_type=F32)
    go += lax.dot_general(zf.astype(BF16), e_peer[:, mine], TN, preferred_element_type=F32)
    gout[...] = go.astype(BF16)


def grads_call(side, us, u_peer, es, e_peer, wi, wo, z, p):
    hidden = wi.shape[1]
    half = us.shape[1] // 2
    return pl.pallas_call(
        grads_body,
        grid=(hidden // TILE,),
        out_shape=(
            jax.ShapeDtypeStruct((half, hidden), BF16),
            jax.ShapeDtypeStruct((hidden, half), BF16),
        ),
        in_specs=[IN_SMEM] + [IN_VMEM] * 8,
        out_specs=[
            pl.BlockSpec((half, TILE), lambda j: (0, j)),
            pl.BlockSpec((TILE, half), lambda j: (j, 0)),
        ],
        compiler_params=params(20),
        name="weight_grads",
    )(side, us, u_peer, es, e_peer, wi, wo, z, p)


def shards(inputs, cotangent, gain, weight_in, weight_out):
    stages = lax.axis_size("pipe")
    ways = lax.axis_size("mp")
    stage = lax.axis_index("pipe")
    part = lax.axis_index("mp")
    replica = lax.axis_index("dp")
    core = lax.rem(part, 2)
    chip = part // 2
    micro, rows, width = inputs.shape
    full = gain.shape[1]
    hidden = weight_in.shape[2]
    ring = ways // 2
    all_rows = micro * rows
    chunk = all_rows // ways

    core_pairs = [(i, i ^ 1) for i in range(ways)]
    dp_pairs = [(0, 1), (1, 0)]

    def turned(i, turn):
        return ((i // 2 + turn) % ring) * 2 + i % 2

    def swap(block):
        return lax.ppermute(block, "mp", core_pairs)

    def spread(block, by):
        out = []
        for d in range(ring):
            pairs = [
                (k * ways + i, ((k + by) % stages) * ways + turned(i, d))
                for k in range(stages)
                for i in range(ways)
            ]
            out.append(lax.ppermute(block, ("pipe", "mp"), pairs))
        return out

    def collect(own, other):
        total = own + swap(other).astype(F32)
        terms = [total[:chunk]]
        for d in range(1, ring):
            slot = ring - d
            block = total[slot * chunk : (slot + 1) * chunk].astype(BF16)
            terms.append(lax.ppermute(block, "mp", [(i, turned(i, d)) for i in range(ways)]))
        return terms

    flags = (jnp.arange(stages, dtype=jnp.int32) == stage).astype(jnp.int32)

    both = jnp.stack([inputs, cotangent])
    both = lax.all_gather(both, "mp", axis=3, tiled=True).reshape(2, ways, chunk, full)

    def slots(array, side):
        places = [side * ring + lax.rem(chip - d + ring, ring) for d in range(ring)]
        return [lax.dynamic_index_in_dim(array, at, 0, keepdims=False) for at in places]

    x_first = slots(both[0], core)
    e_first = slots(both[1], core)
    e_second = slots(both[1], 1 - core)
    wi, wo = load_weights(weight_in[0], weight_out[0])
    z, s, p, n_save, r_save, gg = alloc(
        [(all_rows, hidden)] * 3 + [(chunk, full), (chunk, 128), (8, full)],
        [BF16, BF16, BF16, F32, F32, F32],
    )
    us = jnp.zeros((all_rows, full), BF16)
    es = jnp.zeros((all_rows, full), BF16)

    incoming = x_first
    for t in range(stages):
        last = t == stages - 1
        u_own, n_save, r_save = norm_call(t, flags, incoming, gain, n_save, r_save)
        u_oth = swap(u_own)
        p_own, p_oth, z, s, us = forward_call(t, last, flags, u_own, u_oth, wi, wo, z, s, us)
        if not last:
            t0, t1, t2, t3 = collect(p_own, p_oth)
            total = (t0 + t1.astype(F32)) + (t2.astype(F32) + t3.astype(F32))
            block = (incoming[0].astype(F32) + total).astype(BF16)
            incoming = spread(block, 1)

    u_peer = lax.ppermute(us, "dp", dp_pairs)

    incoming = e_first
    for t in range(stages - 1, -1, -1):
        e_own = jnp.concatenate(incoming, axis=0)
        e_oth = jnp.concatenate(e_second, axis=0) if t == stages - 1 else swap(e_own)
        q_own, q_oth, p, es = backward_call(t, flags, e_own, e_oth, wi, wo, s, p, es)
        if t == 0:
            e_peer = lax.ppermute(es, "dp", dp_pairs)
        block, gg = norm_back_call(
            t, flags, collect(q_own, q_oth), incoming[0], gain, n_save, r_save, gg
        )
        if t > 0:
            incoming = spread(block, -1)

    side = replica.astype(jnp.int32).reshape(1)
    grad_in, grad_out = grads_call(side, us, u_peer, es, e_peer, wi, wo, z, p)
    sums = gg
    sums = sums + lax.ppermute(sums, "dp", dp_pairs)
    sums = sums + swap(sums)
    sums = sums + lax.ppermute(sums, "mp", [(i, i ^ 2) for i in range(ways)])
    sums = sums + lax.ppermute(sums, "mp", [(i, i ^ 4) for i in range(ways)])
    grad_gain = lax.dynamic_slice_in_dim(sums[0:1], part * width, width, 1)
    return (grad_in[None], grad_out[None], grad_gain)


def solution(mesh):
    in_specs = (
        P(None, "dp", "mp"),
        P(None, "dp", "mp"),
        P("pipe", None),
        P("pipe", None, "mp"),
        P("pipe", "mp", None),
    )
    out_specs = (P("pipe", "dp", "mp"), P("pipe", "mp", "dp"), P("pipe", "mp"))
    return jax.shard_map(shards, mesh=mesh, in_specs=in_specs, out_specs=out_specs, check_vma=False)
```

time: 1700 us -> 527 us (0.31)
  waiting for transfers between devices: 987 us -> 218 us
  blocking collectives: 485 us -> 0 us
  starting transfers between devices: 49.2 us -> 199 us
  matrix products: 77.9 us -> 0 us
  Pallas kernels: 0 us -> 49.5 us
  other arithmetic: 43.7 us -> 3.49 us
    reduce_scatter x23 -> x0, waiting for transfers between devices: 940 us -> none  [the longest x11 383 us: backward_turn(): lax.psum_scatter(norm_part, 'mp', scatter_dimension=1, tiled=True)]
    all_gather x22 -> x0, blocking collectives: 313 us -> none  [the longest x11 166 us: forward_turn(): whole_rows = lax.all_gather(segment_input, 'mp', axis=1, tiled=True)]
    psum x12 -> x0, blocking collectives: 172 us -> none  [the longest x11 166 us: backward_turn(): row_dot = lax.psum(jnp.sum(scaled * unit_own, axis=1), 'mp')]
    ppermute x22 -> x137, starting transfers between devices: 49.2 us -> 199 us  [the longest x56 92.7 us: spread(): out.append(lax.ppermute(block, ('pipe', 'mp'), pairs))]
    ppermute x22 -> x137, waiting for transfers between devices: 46.1 us -> 193 us  [the longest x56 79.7 us: spread(): out.append(lax.ppermute(block, ('pipe', 'mp'), pairs))]
    dot_general x18 -> x0, matrix products: 77.9 us -> none  [the longest x4 29.1 us: backward_active(): lax.dot_general(gathered, weight_second, CONTRACT_LAST, preferred_element...]
    pallas_call x0 -> x35, Pallas kernels: none -> 49.5 us  [the longest x1 14.3 us: grads_call(): pl.pallas_call(grads_body, grid=(hidden // TILE,), out_shape=(jax.ShapeDt...]
    all_gather x0 -> x1, waiting for transfers between devices: none -> 25.2 us  [shards(): lax.all_gather(both, 'mp', axis=3, tiled=True).reshape(2, ways, chunk, full)]
  transfers between devices with their start and end apart: 45 -> 138, of which waited for: 45 -> 96; matrix products, arithmetic and copies ran while one was open for 0% -> 0% of each run, Pallas kernels for 0% -> 0%
where the time goes in v1:
time: 527 us; the launch traced here: 518 us
  waiting for transfers between devices  218 us (41%)
  starting transfers between devices  199 us (38%)
  Pallas kernels  49.5 us (9%)
  local copies, waits for them, and re-layouts  32.6 us (6%)
  between operations  15.7 us (3%)
    ppermute x56, starting transfers between devices, spread(): out.append(lax.ppermute(block, ('pipe', 'mp'), pairs))  92.7 us
    ppermute x56, waiting for transfers between devices, spread(): out.append(lax.ppermute(block, ('pipe', 'mp'), pairs))  79.7 us
    ppermute x45, waiting for transfers between devices, collect(): lax.ppermute(block, 'mp', [(i, turned(i, d)) for i in range(ways)])  63.2 us
    ppermute x31, starting transfers between devices, swap(): return lax.ppermute(block, 'mp', core_pairs)  49.4 us
    ppermute x45, starting transfers between devices, collect(): lax.ppermute(block, 'mp', [(i, turned(i, d)) for i in range(ways)])  47.7 us
    ppermute x31, waiting for transfers between devices, swap(): return lax.ppermute(block, 'mp', core_pairs)  32.7 us
    unnamed x59, local copies, waits for them, and re-layouts  28.8 us
    all_gather x1, waiting for transfers between devices, shards(): lax.all_gather(both, 'mp', axis=3, tiled=True).reshape(2, ways, chunk, full)  25.2 us
  transfers between devices with their start and end apart: 138, of which 96 were waited for; matrix products, arithmetic and copies ran while one was open for 0% of the time, Pallas kernels for 0%

profile of v1, /device:TPU:1, one launch (start us, length us, event | category | flops | bytes accessed | tf_op | source)
XLA Modules:
  0.0 518.1 jit_solution(5363206472043865970)
XLA Ops:
  11.5 25.2 %all-gather.2.cloned.1.call-done = bf16[2,4,64,1024]{3,2,1,0:T(8,128)(2,1)} async-done(((bf16[2,4,64,128]{3,2,1,0:T(8,128)(2,1)}), bf16[2,4,64,1024]{3,2,1,0:T(8,128)(2,1)}) %all-gather.2.cloned.1.call-update) | async-done | bytes 1048592 | tf_op jit(solution)/shard_map/all_gather | solution.py:314
  48.2 7.3 %forward_t0.1 = (f32[128,1024]{1,0:T(8,128)S(1)}, bf16[128,1024]{1,0:T(8,128)(2,1)S(1)}, bf16[256,4096]{1,0:T(8,128)(2,1)S(1)}, bf16[256,4096]{1,0:T(8,128)(2,1)S(1)}, bf16[256,1024]{1,0:T(8,128)(2,1)S(1)}) custom-call(s32[8]{0:T(128)S(1)} %compare_convert_fusion.flags, ...), custom_call_target="tpu_custom_call", output_to_operand_aliasing={{2}: (5, {}), {3}: (6, {}), {4}: (7, {})} | custom-call | tf_op jit(solution)/shard_map/forward_t0/pallas_call | solution.py:139
  65.0 5.9 %collective-permute-done.8.a3 = bf16[32,1024]{1,0:T(8,128)(2,1)S(1)} collective-permute-done((bf16[32,1024]{1,0:T(8,128)(2,1)S(1)}, bf16[32,1024]{1,0:T(8,128)(2,1)S(1)}, u32[]{:S(2)}, u32[]{:S(2)}) %collective-permute-start.8) | collective-permute-done | bytes 65568 | tf_op jit(solution)/shard_map/ppermute | solution.py:299
  95.9 5.2 %collective-permute-done.16.a2 = bf16[32,1024]{1,0:T(8,128)(2,1)S(1)} collective-permute-done((bf16[32,1024]{1,0:T(8,128)(2,1)S(1)}, bf16[32,1024]{1,0:T(8,128)(2,1)S(1)}, u32[]{:S(2)}, u32[]{:S(2)}) %collective-permute-start.16) | collective-permute-done | bytes 65568 | tf_op jit(solution)/shard_map/ppermute | solution.py:299
  116.8 6.0 %collective-permute-start.25 = (bf16[32,1024]{1,0:T(8,128)(2,1)S(1)}, bf16[32,1024]{1,0:T(8,128)(2,1)S(1)}, u32[]{:S(2)}, u32[]{:S(2)}) collective-permute-start(bf16[32,1024]{1,0:T(8,128)(2,1)S(1)} %fusion.14), channel_id=1, source_target_pairs={{0,12},{1,13},{2,14},{3,15},{4,8},{5,9},{6,10},{7,11},{8,20},{9,21... | collective-permute-start | bytes 196616 | tf_op jit(solution)/shard_map/ppermute | solution.py:299
  124.7 5.5 %collective-permute-done.24.a1 = bf16[32,1024]{1,0:T(8,128)(2,1)S(1)} collective-permute-done((bf16[32,1024]{1,0:T(8,128)(2,1)S(1)}, bf16[32,1024]{1,0:T(8,128)(2,1)S(1)}, u32[]{:S(2)}, u32[]{:S(2)}) %collective-permute-start.24) | collective-permute-done | bytes 65568 | tf_op jit(solution)/shard_map/ppermute | solution.py:299
  173.0 7.3 %collective-permute-start.41 = (bf16[32,1024]{1,0:T(8,128)(2,1)S(1)}, bf16[32,1024]{1,0:T(8,128)(2,1)S(1)}, u32[]{:S(2)}, u32[]{:S(2)}) collective-permute-start(bf16[32,1024]{1,0:T(8,128)(2,1)S(1)} %fusion.8), channel_id=1, source_target_pairs={{0,8},{1,9},{2,10},{3,11},{4,12},{5,13},{6,14},{7,15},{8,16},{9,17... | collective-permute-start | bytes 196616 | tf_op jit(solution)/shard_map/ppermute | solution.py:299
  204.4 4.7 collective-permute-done.52.a2
  262.9 10.3 %collective-permute-start.69 = (bf16[32,1024]{1,0:T(8,128)(2,1)S(1)}, bf16[32,1024]{1,0:T(8,128)(2,1)S(1)}, u32[]{:S(2)}, u32[]{:S(2)}) collective-permute-start(bf16[32,1024]{1,0:T(8,128)(2,1)S(1)} %get-tuple-element.193), channel_id=1, source_target_pairs={{0,56},{1,57},{2,58},{3,59},{4,60},{5,61},{6,62},{7,63},{8,0},{9,1... | collective-permute-start | bytes 196616 | tf_op jit(solution)/shard_map/ppermute | solution.py:299
  274.6 6.0 %collective-permute-done.70 = bf16[32,1024]{1,0:T(8,128)(2,1)S(1)} collective-permute-done((bf16[32,1024]{1,0:T(8,128)(2,1)S(1)}, bf16[32,1024]{1,0:T(8,128)(2,1)S(1)}, u32[]{:S(2)}, u32[]{:S(2)}) %collective-permute-start.70) | collective-permute-done | bytes 65568 | tf_op jit(solution)/shard_map/ppermute | solution.py:299
  300.6 5.4 %collective-permute-done.79 = bf16[32,1024]{1,0:T(8,128)(2,1)S(1)} collective-permute-done((bf16[32,1024]{1,0:T(8,128)(2,1)S(1)}, bf16[32,1024]{1,0:T(8,128)(2,1)S(1)}, u32[]{:S(2)}, u32[]{:S(2)}) %collective-permute-start.79) | collective-permute-done | bytes 65568 | tf_op jit(solution)/shard_map/ppermute | solution.py:299
  306.0 3.9 collective-permute-start.82
  323.4 4.8 collective-permute-start.89
  329.4 4.1 collective-permute-done.88
  351.7 4.4 collective-permute-start.97
  373.8 4.5 collective-permute-start.105
  379.6 6.2 %collective-permute-done.106 = bf16[32,1024]{1,0:T(8,128)(2,1)S(1)} collective-permute-done((bf16[32,1024]{1,0:T(8,128)(2,1)S(1)}, bf16[32,1024]{1,0:T(8,128)(2,1)S(1)}, u32[]{:S(2)}, u32[]{:S(2)}) %collective-permute-start.106) | collective-permute-done | bytes 65568 | tf_op jit(solution)/shard_map/ppermute | solution.py:299
  398.8 4.1 collective-permute-start.114
  407.4 5.8 %collective-permute-done.115 = bf16[32,1024]{1,0:T(8,128)(2,1)S(1)} collective-permute-done((bf16[32,1024]{1,0:T(8,128)(2,1)S(1)}, bf16[32,1024]{1,0:T(8,128)(2,1)S(1)}, u32[]{:S(2)}, u32[]{:S(2)}) %collective-permute-start.115) | collective-permute-done | bytes 65568 | tf_op jit(solution)/shard_map/ppermute | solution.py:299
  434.8 4.3 collective-permute-done.124
  443.0 6.1 %backward_t0.1 = (f32[128,1024]{1,0:T(8,128)S(1)}, bf16[128,1024]{1,0:T(8,128)(2,1)S(1)}, bf16[256,4096]{1,0:T(8,128)(2,1)S(1)}, bf16[256,1024]{1,0:T(8,128)(2,1)S(1)}) custom-call(s32[8]{0:T(128)S(1)} %compare_convert_fusion.flags, bf16[128,1024]{1,0:T(8,128)(2,1)S(1)} %constant_dynamic-update-slice_fusion.24.e_own, ...), custom_call_target="tpu_custom_call", output_to_operand_aliasing={{2}: (6, {}), {3}: (7, {})} | custom-call | tf_op jit(solution)/shard_map/backward_t0/pallas_call | solution.py:185
  450.8 4.2 collective-permute-start.64
  466.7 12.3 %collective-permute-done.133 = f32[8,1024]{1,0:T(8,128)S(1)} collective-permute-done((f32[8,1024]{1,0:T(8,128)S(1)}, f32[8,1024]{1,0:T(8,128)S(1)}, u32[]{:S(2)}, u32[]{:S(2)}) %collective-permute-start.133) | collective-permute-done | bytes 32800 | tf_op jit(solution)/shard_map/ppermute | solution.py:361
  496.5 14.3 %weight_grads.1 = (bf16[512,4096]{1,0:T(8,128)(2,1)}, bf16[4096,512]{1,0:T(8,128)(2,1)}) custom-call(s32[1]{0:T(128)} %bitcast.side, bf16[256,1024]{1,0:T(8,128)(2,1)S(1)} %get-tuple-element.185.us, bf16[256,1024]{1,0:T(8,128)(2,1)} %collective-permute-done.64.u_peer, bf16[256,1024]{1,0:T(8,128)(2,1)S(1)} %get-tuple-element.232.es, ...), custom_call_target="tpu_custom_call" | custom-call | tf_op jit(solution)/shard_map/weight_grads/pallas_call | solution.py:250
  (413 shorter events, 334.5 us)
Async XLA Ops:
  7.2 29.5 %all-gather.2.cloned.1.call-start = ((), (), s32[]{:S(2)}) async-start(), calls=%async_computation | async-start | bytes 1179648 | tf_op jit(solution)/shard_map/all_gather | solution.py:314
  64.8 8.6 %collective-permute-start.7 = (bf16[32,1024]{1,0:T(8,128)(2,1)S(1)}, bf16[32,1024]{1,0:T(8,128)(2,1)S(1)}, u32[]{:S(2)}, u32[]{:S(2)}) collective-permute-start(bf16[32,1024]{1,0:T(8,128)(2,1)S(1)} %fusion.20), channel_id=1, source_target_pairs={{0,12},{1,13},{2,14},{3,15},{4,8},{5,9},{6,10},{7,11},{8,20},{9,21... | collective-permute-start | bytes 196616 | tf_op jit(solution)/shard_map/ppermute | solution.py:299
  64.9 9.7 %collective-permute-start.6 = (bf16[32,1024]{1,0:T(8,128)(2,1)S(1)}, bf16[32,1024]{1,0:T(8,128)(2,1)S(1)}, u32[]{:S(2)}, u32[]{:S(2)}) collective-permute-start(bf16[32,1024]{1,0:T(8,128)(2,1)S(1)} %fusion.20), channel_id=1, source_target_pairs={{0,10},{1,11},{2,12},{3,13},{4,14},{5,15},{6,8},{7,9},{8,18},{9,19... | collective-permute-start | bytes 196616 | tf_op jit(solution)/shard_map/ppermute | solution.py:299
  65.0 9.7 %collective-permute-start.5 = (bf16[32,1024]{1,0:T(8,128)(2,1)S(1)}, bf16[32,1024]{1,0:T(8,128)(2,1)S(1)}, u32[]{:S(2)}, u32[]{:S(2)}) collective-permute-start(bf16[32,1024]{1,0:T(8,128)(2,1)S(1)} %fusion.20), channel_id=1, source_target_pairs={{0,8},{1,9},{2,10},{3,11},{4,12},{5,13},{6,14},{7,15},{8,16},{9,17... | collective-permute-start | bytes 196616 | tf_op jit(solution)/shard_map/ppermute | solution.py:299
  93.2 8.3 %collective-permute-start.15 = (bf16[32,1024]{1,0:T(8,128)(2,1)S(1)}, bf16[32,1024]{1,0:T(8,128)(2,1)S(1)}, u32[]{:S(2)}, u32[]{:S(2)}) collective-permute-start(bf16[32,1024]{1,0:T(8,128)(2,1)S(1)} %fusion.17), channel_id=1, source_target_pairs={{0,10},{1,11},{2,12},{3,13},{4,14},{5,15},{6,8},{7,9},{8,18},{9,19... | collective-permute-start | bytes 196616 | tf_op jit(solution)/shard_map/ppermute | solution.py:299
  93.2 8.3 %collective-permute-start.14 = (bf16[32,1024]{1,0:T(8,128)(2,1)S(1)}, bf16[32,1024]{1,0:T(8,128)(2,1)S(1)}, u32[]{:S(2)}, u32[]{:S(2)}) collective-permute-start(bf16[32,1024]{1,0:T(8,128)(2,1)S(1)} %fusion.17), channel_id=1, source_target_pairs={{0,8},{1,9},{2,10},{3,11},{4,12},{5,13},{6,14},{7,15},{8,16},{9,17... | collective-permute-start | bytes 196616 | tf_op jit(solution)/shard_map/ppermute | solution.py:299
  145.6 8.4 %collective-permute-start.34 = (bf16[32,1024]{1,0:T(8,128)(2,1)S(1)}, bf16[32,1024]{1,0:T(8,128)(2,1)S(1)}, u32[]{:S(2)}, u32[]{:S(2)}) collective-permute-start(bf16[32,1024]{1,0:T(8,128)(2,1)S(1)} %fusion.11), channel_id=1, source_target_pairs={{0,12},{1,13},{2,14},{3,15},{4,8},{5,9},{6,10},{7,11},{8,20},{9,21... | collective-permute-start | bytes 196616 | tf_op jit(solution)/shard_map/ppermute | solution.py:299
  145.7 8.4 %collective-permute-start.33 = (bf16[32,1024]{1,0:T(8,128)(2,1)S(1)}, bf16[32,1024]{1,0:T(8,128)(2,1)S(1)}, u32[]{:S(2)}, u32[]{:S(2)}) collective-permute-start(bf16[32,1024]{1,0:T(8,128)(2,1)S(1)} %fusion.11), channel_id=1, source_target_pairs={{0,10},{1,11},{2,12},{3,13},{4,14},{5,15},{6,8},{7,9},{8,18},{9,19... | collective-permute-start | bytes 196616 | tf_op jit(solution)/shard_map/ppermute | solution.py:299
  170.3 10.0 %collective-permute-start.44 = (bf16[32,1024]{1,0:T(8,128)(2,1)S(1)}, bf16[32,1024]{1,0:T(8,128)(2,1)S(1)}, u32[]{:S(2)}, u32[]{:S(2)}) collective-permute-start(bf16[32,1024]{1,0:T(8,128)(2,1)S(1)} %fusion.8), channel_id=1, source_target_pairs={{0,14},{1,15},{2,8},{3,9},{4,10},{5,11},{6,12},{7,13},{8,22},{9,23... | collective-permute-start | bytes 196616 | tf_op jit(solution)/shard_map/ppermute | solution.py:299
  170.5 9.8 %collective-permute-start.43 = (bf16[32,1024]{1,0:T(8,128)(2,1)S(1)}, bf16[32,1024]{1,0:T(8,128)(2,1)S(1)}, u32[]{:S(2)}, u32[]{:S(2)}) collective-permute-start(bf16[32,1024]{1,0:T(8,128)(2,1)S(1)} %fusion.8), channel_id=1, source_target_pairs={{0,12},{1,13},{2,14},{3,15},{4,8},{5,9},{6,10},{7,11},{8,20},{9,21... | collective-permute-start | bytes 196616 | tf_op jit(solution)/shard_map/ppermute | solution.py:299
  171.6 8.7 %collective-permute-start.42 = (bf16[32,1024]{1,0:T(8,128)(2,1)S(1)}, bf16[32,1024]{1,0:T(8,128)(2,1)S(1)}, u32[]{:S(2)}, u32[]{:S(2)}) collective-permute-start(bf16[32,1024]{1,0:T(8,128)(2,1)S(1)} %fusion.8), channel_id=1, source_target_pairs={{0,10},{1,11},{2,12},{3,13},{4,14},{5,15},{6,8},{7,9},{8,18},{9,19... | collective-permute-start | bytes 196616 | tf_op jit(solution)/shard_map/ppermute | solution.py:299
  173.0 8.7 %collective-permute-start.41 = (bf16[32,1024]{1,0:T(8,128)(2,1)S(1)}, bf16[32,1024]{1,0:T(8,128)(2,1)S(1)}, u32[]{:S(2)}, u32[]{:S(2)}) collective-permute-start(bf16[32,1024]{1,0:T(8,128)(2,1)S(1)} %fusion.8), channel_id=1, source_target_pairs={{0,8},{1,9},{2,10},{3,11},{4,12},{5,13},{6,14},{7,15},{8,16},{9,17... | collective-permute-start | bytes 196616 | tf_op jit(solution)/shard_map/ppermute | solution.py:299
  262.9 11.7 %collective-permute-start.69 = (bf16[32,1024]{1,0:T(8,128)(2,1)S(1)}, bf16[32,1024]{1,0:T(8,128)(2,1)S(1)}, u32[]{:S(2)}, u32[]{:S(2)}) collective-permute-start(bf16[32,1024]{1,0:T(8,128)(2,1)S(1)} %get-tuple-element.193), channel_id=1, source_target_pairs={{0,56},{1,57},{2,58},{3,59},{4,60},{5,61},{6,62},{7,63},{8,0},{9,1... | collective-permute-start | bytes 196616 | tf_op jit(solution)/shard_map/ppermute | solution.py:299
  296.5 9.5 %collective-permute-start.81 = (bf16[32,1024]{1,0:T(8,128)(2,1)S(1)}, bf16[32,1024]{1,0:T(8,128)(2,1)S(1)}, u32[]{:S(2)}, u32[]{:S(2)}) collective-permute-start(bf16[32,1024]{1,0:T(8,128)(2,1)S(1)} %get-tuple-element.199), channel_id=1, source_target_pairs={{0,62},{1,63},{2,56},{3,57},{4,58},{5,59},{6,60},{7,61},{8,6},{9,7... | collective-permute-start | bytes 196616 | tf_op jit(solution)/shard_map/ppermute | solution.py:299
  321.0 8.4 %collective-permute-start.87 = (bf16[32,1024]{1,0:T(8,128)(2,1)S(1)}, bf16[32,1024]{1,0:T(8,128)(2,1)S(1)}, u32[]{:S(2)}, u32[]{:S(2)}) collective-permute-start(bf16[32,1024]{1,0:T(8,128)(2,1)S(1)} %get-tuple-element.205), channel_id=1, source_target_pairs={{0,56},{1,57},{2,58},{3,59},{4,60},{5,61},{6,62},{7,63},{8,0},{9,1... | collective-permute-start | bytes 196616 | tf_op jit(solution)/shard_map/ppermute | solution.py:299
  322.7 10.8 %collective-permute-start.90 = (bf16[32,1024]{1,0:T(8,128)(2,1)S(1)}, bf16[32,1024]{1,0:T(8,128)(2,1)S(1)}, u32[]{:S(2)}, u32[]{:S(2)}) collective-permute-start(bf16[32,1024]{1,0:T(8,128)(2,1)S(1)} %get-tuple-element.205), channel_id=1, source_target_pairs={{0,62},{1,63},{2,56},{3,57},{4,58},{5,59},{6,60},{7,61},{8,6},{9,7... | collective-permute-start | bytes 196616 | tf_op jit(solution)/shard_map/ppermute | solution.py:299
  323.4 10.1 %collective-permute-start.89 = (bf16[32,1024]{1,0:T(8,128)(2,1)S(1)}, bf16[32,1024]{1,0:T(8,128)(2,1)S(1)}, u32[]{:S(2)}, u32[]{:S(2)}) collective-permute-start(bf16[32,1024]{1,0:T(8,128)(2,1)S(1)} %get-tuple-element.205), channel_id=1, source_target_pairs={{0,60},{1,61},{2,62},{3,63},{4,56},{5,57},{6,58},{7,59},{8,4},{9,5... | collective-permute-start | bytes 196616 | tf_op jit(solution)/shard_map/ppermute | solution.py:299
  398.8 8.6 %collective-permute-start.114 = (bf16[32,1024]{1,0:T(8,128)(2,1)S(1)}, bf16[32,1024]{1,0:T(8,128)(2,1)S(1)}, u32[]{:S(2)}, u32[]{:S(2)}) collective-permute-start(bf16[32,1024]{1,0:T(8,128)(2,1)S(1)} %get-tuple-element.223), channel_id=1, source_target_pairs={{0,56},{1,57},{2,58},{3,59},{4,60},{5,61},{6,62},{7,63},{8,0},{9,1... | collective-permute-start | bytes 196616 | tf_op jit(solution)/shard_map/ppermute | solution.py:299
  402.9 10.3 %collective-permute-start.117 = (bf16[32,1024]{1,0:T(8,128)(2,1)S(1)}, bf16[32,1024]{1,0:T(8,128)(2,1)S(1)}, u32[]{:S(2)}, u32[]{:S(2)}) collective-permute-start(bf16[32,1024]{1,0:T(8,128)(2,1)S(1)} %get-tuple-element.223), channel_id=1, source_target_pairs={{0,62},{1,63},{2,56},{3,57},{4,58},{5,59},{6,60},{7,61},{8,6},{9,7... | collective-permute-start | bytes 196616 | tf_op jit(solution)/shard_map/ppermute | solution.py:299
  429.4 9.8 %collective-permute-start.126 = (bf16[32,1024]{1,0:T(8,128)(2,1)S(1)}, bf16[32,1024]{1,0:T(8,128)(2,1)S(1)}, u32[]{:S(2)}, u32[]{:S(2)}) collective-permute-start(bf16[32,1024]{1,0:T(8,128)(2,1)S(1)} %get-tuple-element.229), channel_id=1, source_target_pairs={{0,62},{1,63},{2,56},{3,57},{4,58},{5,59},{6,60},{7,61},{8,6},{9,7... | collective-permute-start | bytes 196616 | tf_op jit(solution)/shard_map/ppermute | solution.py:299
  430.2 8.9 %collective-permute-start.125 = (bf16[32,1024]{1,0:T(8,128)(2,1)S(1)}, bf16[32,1024]{1,0:T(8,128)(2,1)S(1)}, u32[]{:S(2)}, u32[]{:S(2)}) collective-permute-start(bf16[32,1024]{1,0:T(8,128)(2,1)S(1)} %get-tuple-element.229), channel_id=1, source_target_pairs={{0,60},{1,61},{2,62},{3,63},{4,56},{5,57},{6,58},{7,59},{8,4},{9,5... | collective-permute-start | bytes 196616 | tf_op jit(solution)/shard_map/ppermute | solution.py:299
  450.8 37.4 %collective-permute-start.64 = (bf16[256,1024]{1,0:T(8,128)(2,1)S(1)}, bf16[256,1024]{1,0:T(8,128)(2,1)}, u32[]{:S(2)}, u32[]{:S(2)}) collective-permute-start(bf16[256,1024]{1,0:T(8,128)(2,1)S(1)} %get-tuple-element.185.us), channel_id=1, source_target_pairs={{0,64},{64,0},{1,65},{65,1},{2,66},{66,2},{3,67},{67,3},{4,68},{68... | collective-permute-start | bytes 1572872 | tf_op jit(solution)/shard_map/ppermute | solution.py:343
  454.9 33.3 %collective-permute-start.128 = (bf16[256,1024]{1,0:T(8,128)(2,1)S(1)}, bf16[256,1024]{1,0:T(8,128)(2,1)}, u32[]{:S(2)}, u32[]{:S(2)}) collective-permute-start(bf16[256,1024]{1,0:T(8,128)(2,1)S(1)} %get-tuple-element.232.es), channel_id=1, source_target_pairs={{0,64},{64,0},{1,65},{65,1},{2,66},{66,2},{3,67},{67,3},{4,68},{68... | collective-permute-start | bytes 1572872 | tf_op jit(solution)/shard_map/ppermute | solution.py:351
  464.0 15.0 %collective-permute-start.133 = (f32[8,1024]{1,0:T(8,128)S(1)}, f32[8,1024]{1,0:T(8,128)S(1)}, u32[]{:S(2)}, u32[]{:S(2)}) collective-permute-start(f32[8,1024]{1,0:T(8,128)S(1)} %get-tuple-element.240), channel_id=1, source_target_pairs={{0,64},{64,0},{1,65},{65,1},{2,66},{66,2},{3,67},{67,3},{4,68},{68... | collective-permute-start | bytes 98312 | tf_op jit(solution)/shard_map/ppermute | solution.py:361
  (133 other events, 991.0 us)
Sparse Core Ops, SparseCore 0:
  9.7 26.9 all-gather.1

commit v2 on v1

v2 whole, which is shorter than its diff:
```python
import functools
import math

import jax
import jax.numpy as jnp
from jax import lax
from jax.experimental import pallas as pl
from jax.experimental.pallas import tpu as pltpu
from jax.sharding import PartitionSpec as P

GELU_COEF = math.sqrt(2.0 / math.pi)
CUBIC_COEF = 0.044715
NORM_EPS = 1e-06
BF16 = jnp.bfloat16
F32 = jnp.float32
NT = (((1,), (1,)), ((), ()))
TN = (((0,), (0,)), ((), ()))
MIB = 2**20
FWD_TILE = 256
BWD_TILE = 1024
GRAD_TILE = 512
REPLICA, CORE, CHIP = 9, 10, 11
VMEM = pltpu.VMEM
IN_VMEM = pl.BlockSpec(memory_space=pltpu.VMEM)
IN_SMEM = pl.BlockSpec(memory_space=pltpu.SMEM)
ANYWHERE = pl.BlockSpec(memory_space=pl.ANY)
IN_HBM = pl.BlockSpec(memory_space=pltpu.HBM)


def params(mib):
    return pltpu.CompilerParams(vmem_limit_bytes=int(mib * MIB))


def gelu_both(a):
    a2 = a * a
    t = jnp.tanh(a * (GELU_COEF + (GELU_COEF * CUBIC_COEF) * a2))
    h = 0.5 + 0.5 * t
    z = a * h
    slope = h + (a * (0.5 - 0.5 * t * t)) * (GELU_COEF + (3.0 * GELU_COEF * CUBIC_COEF) * a2)
    return z, slope


def load_body(after, wi, wo, wi_out, wo_out, z, s, p, n_save, r_save, gg, sems):
    first = pltpu.make_async_copy(wi.at[0], wi_out, sems.at[0])
    second = pltpu.make_async_copy(wo.at[0], wo_out, sems.at[1])
    first.start()
    second.start()
    gg[...] = jnp.zeros_like(gg)
    first.wait()
    second.wait()


def load_weights(after, wi, wo, saves):
    return pl.pallas_call(
        load_body,
        out_shape=(VMEM(wi.shape[1:], wi.dtype), VMEM(wo.shape[1:], wo.dtype))
        + tuple(VMEM(shape, kind) for shape, kind in saves),
        in_specs=[ANYWHERE] + [IN_HBM] * 2,
        out_specs=[IN_VMEM] * (2 + len(saves)),
        scratch_shapes=[pltpu.SemaphoreType.DMA((2,))],
        compiler_params=params(38),
        name="load_weights",
    )(after, wi, wo)


def pick_body(ring, sides, info, parts, *outs):
    chunk, width = parts.shape[2], parts.shape[3]
    for side, out in zip(sides, outs):
        half = info[CORE] if side == 0 else 1 - info[CORE]
        for d in range(ring):
            at = half * ring + lax.rem(info[CHIP] - d + ring, ring)
            for k in range(parts.shape[0]):
                out[d * chunk : (d + 1) * chunk, k * width : (k + 1) * width] = parts[k, at]


def pick_call(info, parts, ring, sides, name):
    ways, _, chunk, width = parts.shape
    return pl.pallas_call(
        functools.partial(pick_body, ring, sides),
        out_shape=(jax.ShapeDtypeStruct((ring * chunk, ways * width), BF16),) * len(sides),
        in_specs=[IN_SMEM, IN_VMEM],
        out_specs=[IN_VMEM] * len(sides),
        compiler_params=params(4),
        name=name,
    )(info, parts)


def after_body(x, tie, out):
    out[...] = x[...]


def after_call(x, tie, name):
    return pl.pallas_call(
        after_body,
        out_shape=jax.ShapeDtypeStruct(x.shape, x.dtype),
        in_specs=[IN_VMEM, ANYWHERE],
        out_specs=IN_VMEM,
        compiler_params=params(1),
        name=name,
    )(x, tie)


def total_of(pieces):
    vals = [piece[...].astype(F32) for piece in pieces]
    while len(vals) > 1:
        vals = [a + b for a, b in zip(vals[::2], vals[1::2])]
    return vals[0]


def norm_body(t, count, ties, info, *refs):
    pieces, gain = refs[:count], refs[count]
    u_out, x_out, n_save, r_save = refs[count + 3 + ties :]
    chunk = x_out.shape[0]

    @pl.when(info[t] > 0)
    def _():
        for d in range(4):
            x = (pieces[d][...] if count == 4 else pieces[0][d * chunk : (d + 1) * chunk, :]).astype(F32)
            r = lax.rsqrt(jnp.mean(x * x, axis=1, keepdims=True) + NORM_EPS)
            n = x * r
            u_out[d * chunk : (d + 1) * chunk, :] = (n * gain[...]).astype(BF16)
            if d == 0:
                x_out[...] = x
                n_save[...] = n
                r_save[...] = jnp.broadcast_to(r, r_save.shape)


def norm_call(t, info, pieces, gain, n_save, r_save, ties):
    count = len(pieces)
    chunk, width = n_save.shape
    return pl.pallas_call(
        functools.partial(norm_body, t, count, len(ties)),
        out_shape=(
            jax.ShapeDtypeStruct((4 * chunk, width), BF16),
            VMEM((chunk, width), F32),
            VMEM(n_save.shape, F32),
            VMEM(r_save.shape, F32),
        ),
        in_specs=[IN_SMEM] + [IN_VMEM] * (count + 3) + [ANYWHERE] * len(ties),
        out_specs=[IN_VMEM] * 4,
        input_output_aliases={count + 2: 2, count + 3: 3},
        compiler_params=params(4),
        name=f"norm_t{t}",
    )(info, *pieces, gain, n_save, r_save, *ties)


def forward_body(t, side, last, info, u, wi, wo, z_in, s_in, out, z, s, acc):
    rows = u.shape[0]

    @pl.when(info[t] > 0)
    def _():
        here = slice(side * rows, (side + 1) * rows)
        for j in range(wi.shape[1] // FWD_TILE):
            cols = slice(j * FWD_TILE, (j + 1) * FWD_TILE)
            a = jnp.dot(u[...], wi[:, cols], preferred_element_type=F32)
            zf, slope = gelu_both(a)
            zb = zf.astype(BF16)
            z[here, cols] = zb
            s[here, cols] = slope.astype(BF16)
            if not last:
                d = jnp.dot(zb, wo[cols, :], preferred_element_type=F32)
                if j == 0:
                    acc[...] = d
                else:
                    acc[...] += d
        if not last:
            out[...] = acc[...].astype(out.dtype)


def forward_call(t, side, last, info, u, wi, wo, z, s):
    shape = u.shape
    return pl.pallas_call(
        functools.partial(forward_body, t, side, last),
        out_shape=(
            VMEM(shape, F32) if side == 0 else jax.ShapeDtypeStruct(shape, BF16),
            VMEM(z.shape, BF16),
            VMEM(s.shape, BF16),
        ),
        in_specs=[IN_SMEM] + [IN_VMEM] * 5,
        out_specs=[IN_VMEM] * 3,
        scratch_shapes=[VMEM(shape, F32)],
        input_output_aliases={4: 1, 5: 2},
        compiler_params=params(12),
        name=f"forward_t{t}_s{side}",
    )(info, u, wi, wo, z, s)


def backward_body(t, ties, info, e_own, e_oth, wi, wo, s, p_in, *refs):
    q_own, q_oth, p, acc = refs[ties:]
    half = e_own.shape[0]

    @pl.when(info[t] > 0)
    def _():
        e = jnp.concatenate([e_own[...], e_oth[...]], axis=0)
        for j in range(wi.shape[1] // BWD_TILE):
            cols = slice(j * BWD_TILE, (j + 1) * BWD_TILE)
            dz = lax.dot_general(e, wo[cols, :], NT, preferred_element_type=F32)
            pb = (dz * s[:, cols].astype(F32)).astype(BF16)
            p[:, cols] = pb
            d = lax.dot_general(pb, wi[:, cols], NT, preferred_element_type=F32)
            if j == 0:
                acc[...] = d
            else:
                acc[...] += d
        q_own[...] = acc[:half]
        q_oth[...] = acc[half:].astype(BF16)


def backward_call(t, info, e_own, e_oth, wi, wo, s, p, ties):
    shape = e_own.shape
    return pl.pallas_call(
        functools.partial(backward_body, t, len(ties)),
        out_shape=(VMEM(shape, F32), jax.ShapeDtypeStruct(shape, BF16), VMEM(p.shape, BF16)),
        in_specs=[IN_SMEM] + [IN_VMEM] * 6 + [ANYWHERE] * len(ties),
        out_specs=[IN_VMEM] * 3,
        scratch_shapes=[VMEM((2 * shape[0], shape[1]), F32)],
        input_output_aliases={6: 2},
        compiler_params=params(14),
        name=f"backward_t{t}",
    )(info, e_own, e_oth, wi, wo, s, p, *ties)


def norm_back_body(t, info, total, q1, q2, q3, g, gain, n_save, r_save, gg_in, *refs):
    out, gg = refs[-2:]
    chunk, width = out.shape

    @pl.when(info[t] > 0)
    def _():
        q = (total[:chunk, :] + q1[...].astype(F32)) + (q2[...].astype(F32) + q3[...].astype(F32))
        n = n_save[...]
        r = r_save[:, 0:1]
        qn = q * n
        gg[0:1, :] = jnp.sum(qn, axis=0, keepdims=True)
        dot = jnp.sum(qn * gain[...], axis=1, keepdims=True) / width
        back = r * (q * gain[...] - n * dot)
        out[...] = (back + g[:chunk, :].astype(F32)).astype(BF16)


def norm_back_call(t, info, terms, g, gain, n_save, r_save, gg, ties):
    return pl.pallas_call(
        functools.partial(norm_back_body, t),
        out_shape=(jax.ShapeDtypeStruct(n_save.shape, BF16), VMEM(gg.shape, F32)),
        in_specs=[IN_SMEM] + [IN_VMEM] * 9 + [ANYWHERE] * len(ties),
        out_specs=[IN_VMEM] * 2,
        input_output_aliases={9: 1},
        compiler_params=params(4),
        name=f"norm_back_t{t}",
    )(info, *terms, g, gain, n_save, r_save, gg, *ties)


def grads_body(groups, base, ties, info, *refs):
    us, up, es, ep = (refs[k * groups : (k + 1) * groups] for k in range(4))
    wi, wo, z, p = refs[4 * groups : 4 * groups + 4]
    gin, gout, *done = refs[4 * groups + 4 + ties :]
    if done:
        done[0][...] = jnp.zeros_like(done[0])
    tile = gin.shape[1]
    half = gin.shape[0]
    cols = pl.ds(pl.multiple_of((base + pl.program_id(0)) * tile, tile), tile)
    mine = pl.ds(pl.multiple_of(info[REPLICA] * half, half), half)

    def rows(parts, at):
        return jnp.concatenate([part[:, at] for part in parts], axis=0)

    every = slice(None)
    a = jnp.dot(rows(up, every), wi[:, cols], preferred_element_type=F32)
    zf, slope = gelu_both(a)
    dz = lax.dot_general(rows(ep, every), wo[cols, :], NT, preferred_element_type=F32)
    p_all = jnp.concatenate([p[:, cols], (dz * slope).astype(BF16)], axis=0)
    z_all = jnp.concatenate([z[:, cols], zf.astype(BF16)], axis=0)
    u_half = rows(us + up, mine)
    e_half = rows(es + ep, mine)
    gin[...] = lax.dot_general(u_half, p_all, TN, preferred_element_type=F32).astype(BF16)
    gout[...] = lax.dot_general(z_all, e_half, TN, preferred_element_type=F32).astype(BF16)


def grads_call(which, info, us, up, es, ep, wi, wo, z, p, ties):
    groups = len(us)
    hidden = wi.shape[1]
    half = us[0].shape[1] // 2
    steps = hidden // GRAD_TILE // 2
    base = which * steps
    return pl.pallas_call(
        functools.partial(grads_body, groups, base, len(ties)),
        grid=(steps,),
        out_shape=(
            jax.ShapeDtypeStruct((half, hidden), BF16),
            jax.ShapeDtypeStruct((hidden, half), BF16),
        )
        + (() if ties else (jax.ShapeDtypeStruct((8, 128), F32),)),
        in_specs=[IN_SMEM] + [IN_VMEM] * (4 * groups + 4) + [IN_HBM] * len(ties),
        out_specs=[
            pl.BlockSpec((half, GRAD_TILE), lambda j: (0, base + j)),
            pl.BlockSpec((GRAD_TILE, half), lambda j: (base + j, 0)),
        ]
        + ([] if ties else [IN_VMEM]),
        input_output_aliases={4 * groups + 5: 0, 4 * groups + 6: 1} if ties else {},
        compiler_params=params(14),
        cost_estimate=pl.CostEstimate(
            flops=2**33, bytes_accessed=2**23, transcendentals=0
        ),
        name=f"weight_grads_{which}",
    )(info, *us, *up, *es, *ep, wi, wo, z, p, *ties)


def quarters_body(ring, info, gg, *outs):
    width = outs[0].shape[1]
    for d in range(ring):
        at = lax.rem(info[CHIP] + d, ring) * width
        outs[d][...] = gg[:, pl.ds(pl.multiple_of(at, width), width)]


def quarters_call(info, gg, ring):
    width = gg.shape[1] // ring
    return pl.pallas_call(
        functools.partial(quarters_body, ring),
        out_shape=(jax.ShapeDtypeStruct((gg.shape[0], width), F32),) * ring,
        in_specs=[IN_SMEM, IN_VMEM],
        out_specs=[IN_VMEM] * ring,
        compiler_params=params(1),
        name="gain_quarters",
    )(info, gg)


def shares_body(count, info, *refs):
    kept, sent, total = refs[count], refs[count + 1], refs[count + 2]
    width = kept.shape[1]
    total[...] = total_of(refs[:count])
    core = info[CORE]
    kept[...] = total[:, pl.ds(pl.multiple_of(core * width, width), width)]
    sent[...] = total[:, pl.ds(pl.multiple_of((1 - core) * width, width), width)]


def shares_call(info, pieces):
    rows, width = pieces[0].shape
    return pl.pallas_call(
        functools.partial(shares_body, len(pieces)),
        out_shape=(jax.ShapeDtypeStruct((rows, width // 2), F32),) * 2,
        in_specs=[IN_SMEM] + [IN_VMEM] * len(pieces),
        out_specs=[IN_VMEM] * 2,
        scratch_shapes=[VMEM((rows, width), F32)],
        compiler_params=params(1),
        name="gain_shares",
    )(info, *pieces)


def pair_body(a, b, out):
    out[...] = a[...] + b[...]


def pair_call(a, b, name):
    return pl.pallas_call(
        pair_body,
        out_shape=jax.ShapeDtypeStruct(a.shape, F32),
        in_specs=[IN_VMEM] * 2,
        out_specs=IN_VMEM,
        compiler_params=params(1),
        name=name,
    )(a, b)


def shards(inputs, cotangent, gain, weight_in, weight_out):
    stages = lax.axis_size("pipe")
    ways = lax.axis_size("mp")
    stage = lax.axis_index("pipe")
    part = lax.axis_index("mp")
    replica = lax.axis_index("dp")
    micro, rows, width = inputs.shape
    full = gain.shape[1]
    hidden = weight_in.shape[2]
    ring = ways // 2
    all_rows = micro * rows
    chunk = all_rows // ways
    half = all_rows // 2

    core_pairs = [(i, i ^ 1) for i in range(ways)]
    dp_pairs = [(0, 1), (1, 0)]

    def turned(i, turn):
        return ((i // 2 + turn) % ring) * 2 + i % 2

    def swap(block):
        return lax.ppermute(block, "mp", core_pairs)

    def trade(block):
        return lax.ppermute(block, "dp", dp_pairs)

    def spread(block, by):
        out = []
        for d in range(ring):
            pairs = [
                (k * ways + i, ((k + by) % stages) * ways + turned(i, d))
                for k in range(stages)
                for i in range(ways)
            ]
            out.append(lax.ppermute(block, ("pipe", "mp"), pairs))
        return out

    def collect(own, other):
        total = own + swap(other).astype(F32)
        terms = [total]
        for d in range(1, ring):
            slot = ring - d
            block = total[slot * chunk : (slot + 1) * chunk].astype(BF16)
            terms.append(lax.ppermute(block, "mp", [(i, turned(i, d)) for i in range(ways)]))
        return terms

    place = jnp.arange(16, dtype=jnp.int32)
    info = (place == stage).astype(jnp.int32) * (place < stages).astype(jnp.int32)
    info = jnp.where(place == REPLICA, replica.astype(jnp.int32), info)
    info = jnp.where(place == CORE, (part & 1).astype(jnp.int32), info)
    info = jnp.where(place == CHIP, (part >> 1).astype(jnp.int32), info)

    def chosen(t, new, old):
        return jnp.where((info[t : t + 1] > 0)[:, None], new, old)

    def gathered(array):
        return lax.all_gather(array.reshape(ways, chunk, width), "mp", axis=0, tiled=False)

    (x_first,) = pick_call(info, gathered(inputs), ring, (0,), "pick_rows")
    wi, wo, z, s, p, n_save, r_save, gg = load_weights(
        x_first,
        weight_in,
        weight_out,
        [((all_rows, hidden), BF16)] * 3 + [((chunk, full), F32), ((chunk, 128), F32), ((8, full), F32)],
    )
    us = jnp.zeros((half, full), BF16)
    incoming = [x_first]
    ties = []
    for t in range(stages):
        last = t == stages - 1
        u_own, x_own, n_save, r_save = norm_call(t, info, incoming, gain, n_save, r_save, ties)
        u_oth = swap(u_own)
        p_own, z, s = forward_call(t, 0, last, info, u_own, wi, wo, z, s)
        p_oth, z, s = forward_call(t, 1, last, info, u_oth, wi, wo, z, s)
        us = chosen(t, u_own, us)
        if not last:
            t0, t1, t2, t3 = collect(p_own, p_oth)
            total = (t0[:chunk] + t1.astype(F32)) + (t2.astype(F32) + t3.astype(F32))
            block = (x_own + total).astype(BF16)
            incoming = spread(block, 1)
            ties = []
            if t == 1:
                late = after_call(cotangent, block, "hold_cotangent")
                e_first, e_second = pick_call(info, gathered(late), ring, (0, 1), "pick_cotangent")
                ties = [e_first]

    es = jnp.zeros((half, full), BF16)
    for t in range(stages - 1, -1, -1):
        if t == stages - 1:
            e_own, e_oth, g = e_first, e_second, e_first
        else:
            e_own, g = jnp.concatenate(incoming, axis=0), incoming[0]
            e_oth = swap(e_own)
        es = chosen(t, e_own, es)
        if t == 0:
            ep = trade(es)
        q_own, q_oth, p = backward_call(
            t, info, e_own, e_oth, wi, wo, s, p, us + up if t == stages - 2 else []
        )
        terms = collect(q_own, q_oth)
        ties = []
        if t == 0:
            es = [es, swap(es)]
            ep = [ep, swap(ep)]
            first = grads_call(0, info, us, up, es, ep, wi, wo, z, p, [])
            *first, done = first
            ties = [done]
        block, gg = norm_back_call(t, info, terms, g, gain, n_save, r_save, gg, ties)
        if t > 0:
            incoming = spread(block, -1)
        if t == stages - 1:
            us = after_call(us, block, "hold_rows")
            us = [us, swap(us)]
            up = trade(us[0])
            up = [up, swap(up)]

    mine, *theirs = quarters_call(info, gg, ring)
    shares = [mine] + [
        lax.ppermute(block, "mp", [(i, turned(i, d + 1)) for i in range(ways)])
        for d, block in enumerate(theirs)
    ]
    kept, sent = shares_call(info, shares)
    share = pair_call(kept, swap(sent), "gain_cores")
    grad_in, grad_out = grads_call(1, info, us, up, es, ep, wi, wo, z, p, list(first) + [share])
    grad_gain = pair_call(share, trade(share), "gain_replicas")[0:1]
    return (grad_in[None], grad_out[None], grad_gain)


def solution(mesh):
    in_specs = (
        P(None, "dp", "mp"),
        P(None, "dp", "mp"),
        P("pipe", None),
        P("pipe", None, "mp"),
        P("pipe", "mp", None),
    )
    out_specs = (P("pipe", "dp", "mp"), P("pipe", "mp", "dp"), P("pipe", "mp"))
    return jax.shard_map(shards, mesh=mesh, in_specs=in_specs, out_specs=out_specs, check_vma=False)
```

time: 527 us -> 477 us (0.905)
  the two profiles are of different devices: /device:TPU:1 before, /device:TPU:31 now
where the time goes in v2:
time: 477 us; the launch traced here: 469 us
  starting transfers between devices  208 us (44%)
  waiting for transfers between devices  159 us (33%)
  Pallas kernels  60.9 us (13%)
  blocking collectives  29.2 us (6%)
  between operations  7.33 us (2%)
    ppermute x56, starting transfers between devices, spread(): out.append(lax.ppermute(block, ('pipe', 'mp'), pairs))  103 us
    ppermute x56, waiting for transfers between devices, spread(): out.append(lax.ppermute(block, ('pipe', 'mp'), pairs))  66 us
    ppermute x45, starting transfers between devices, collect(): lax.ppermute(block, 'mp', [(i, turned(i, d)) for i in range(ways)])  50.1 us
    ppermute x35, starting transfers between devices, swap(): return lax.ppermute(block, 'mp', core_pairs)  47.8 us
    ppermute x45, waiting for transfers between devices, collect(): lax.ppermute(block, 'mp', [(i, turned(i, d)) for i in range(ways)])  47.2 us
    all_gather x2, blocking collectives, gathered(): lax.all_gather(array.reshape(ways, chunk, width), 'mp', axis=0, tiled=False)  29.2 us
    ppermute x35, waiting for transfers between devices, swap(): return lax.ppermute(block, 'mp', core_pairs)  28.3 us
    pallas_call x16, Pallas kernels, forward_call(): pl.pallas_call(functools.partial(forward_body, t, side, last), out_shape=...  18.7 us
  transfers between devices with their start and end apart: 142, of which 89 were waited for; matrix products, arithmetic and copies ran while one was open for 0% of the time, Pallas kernels for 5%

profile of v2, /device:TPU:31, one launch (start us, length us, event | category | flops | bytes accessed | tf_op | source)
XLA Modules:
  0.0 469.3 jit_solution(610276873710441572)
XLA Ops:
  0.6 13.8 %all_gather.6.parts = bf16[8,8,32,128]{3,2,1,0:T(8,128)(2,1)S(1)} all-gather(bf16[1,8,32,128]{3,2,1,0:T(8,128)(2,1)} %bitcast.13), channel_id=1, replica_groups=mesh['dp'=2,'pipe'=8,'mp'=8] {'mp'}, dimensions={0}, use_global_device_ids=true | all-gather | bytes 589824 | tf_op jit(solution)/shard_map/all_gather | solution.py:418
  15.8 5.8 %load_weights.1 = (bf16[1024,4096]{1,0:T(8,128)(2,1)S(1)}, bf16[4096,1024]{1,0:T(8,128)(2,1)S(1)}, bf16[256,4096]{1,0:T(8,128)(2,1)S(1)}, bf16[256,4096]{1,0:T(8...) custom-call(bf16[128,1024]{1,0:T(8,128)(2,1)} %copy-done, ...), custom_call_target="tpu_custom_call" | custom-call | tf_op jit(solution)/shard_map/load_weights/pallas_call | solution.py:54
  57.6 4.9 %collective-permute-start.17 = (bf16[32,1024]{1,0:T(8,128)(2,1)S(1)}, bf16[32,1024]{1,0:T(8,128)(2,1)S(1)}, u32[]{:S(2)}, u32[]{:S(2)}) collective-permute-start(bf16[32,1024]{1,0:T(8,128)(2,1)S(1)} %fusion.17.tie), channel_id=1, source_target_pairs={{0,14},{1,15},{2,8},{3,9},{4,10},{5,11},{6,12},{7,13},{8,22},{9,23... | collective-permute-start | bytes 196616 | tf_op jit(solution)/shard_map/ppermute | solution.py:396
  68.9 15.4 %all_gather.7.parts = bf16[8,8,32,128]{3,2,1,0:T(8,128)(2,1)S(1)} all-gather(bf16[1,8,32,128]{3,2,1,0:T(8,128)(2,1)S(1)} %bitcast.12), channel_id=1, replica_groups=mesh['dp'=2,'pipe'=8,'mp'=8] {'mp'}, dimensions={0}, use_global_device_ids=true | all-gather | bytes 589824 | tf_op jit(solution)/shard_map/all_gather | solution.py:418
  98.2 5.2 %collective-permute-start.25 = (bf16[32,1024]{1,0:T(8,128)(2,1)S(1)}, bf16[32,1024]{1,0:T(8,128)(2,1)S(1)}, u32[]{:S(2)}, u32[]{:S(2)}) collective-permute-start(bf16[32,1024]{1,0:T(8,128)(2,1)S(1)} %fusion.14), channel_id=1, source_target_pairs={{0,12},{1,13},{2,14},{3,15},{4,8},{5,9},{6,10},{7,11},{8,20},{9,21... | collective-permute-start | bytes 196616 | tf_op jit(solution)/shard_map/ppermute | solution.py:396
  152.1 7.6 %collective-permute-start.44 = (bf16[32,1024]{1,0:T(8,128)(2,1)S(1)}, bf16[32,1024]{1,0:T(8,128)(2,1)S(1)}, u32[]{:S(2)}, u32[]{:S(2)}) collective-permute-start(bf16[32,1024]{1,0:T(8,128)(2,1)S(1)} %fusion.8), channel_id=1, source_target_pairs={{0,14},{1,15},{2,8},{3,9},{4,10},{5,11},{6,12},{7,13},{8,22},{9,23... | collective-permute-start | bytes 196616 | tf_op jit(solution)/shard_map/ppermute | solution.py:396
  178.0 5.0 %collective-permute-done.49 = bf16[32,1024]{1,0:T(8,128)(2,1)S(1)} collective-permute-done((bf16[32,1024]{1,0:T(8,128)(2,1)S(1)}, bf16[32,1024]{1,0:T(8,128)(2,1)S(1)}, u32[]{:S(2)}, u32[]{:S(2)}) %collective-permute-start.49) | collective-permute-done | bytes 65568 | tf_op jit(solution)/shard_map/ppermute | solution.py:405
  184.2 6.0 %collective-permute-start.52 = (bf16[32,1024]{1,0:T(8,128)(2,1)S(1)}, bf16[32,1024]{1,0:T(8,128)(2,1)S(1)}, u32[]{:S(2)}, u32[]{:S(2)}) collective-permute-start(bf16[32,1024]{1,0:T(8,128)(2,1)S(1)} %fusion.5), channel_id=1, source_target_pairs={{0,12},{1,13},{2,14},{3,15},{4,8},{5,9},{6,10},{7,11},{8,20},{9,21... | collective-permute-start | bytes 196616 | tf_op jit(solution)/shard_map/ppermute | solution.py:396
  212.3 5.4 %collective-permute-start.60 = (bf16[32,1024]{1,0:T(8,128)(2,1)S(1)}, bf16[32,1024]{1,0:T(8,128)(2,1)S(1)}, u32[]{:S(2)}, u32[]{:S(2)}) collective-permute-start(bf16[32,1024]{1,0:T(8,128)(2,1)S(1)} %fusion.2), channel_id=1, source_target_pairs={{0,10},{1,11},{2,12},{3,13},{4,14},{5,15},{6,8},{7,9},{8,18},{9,19... | collective-permute-start | bytes 196616 | tf_op jit(solution)/shard_map/ppermute | solution.py:396
  242.3 11.4 %collective-permute-start.72 = (bf16[32,1024]{1,0:T(8,128)(2,1)S(1)}, bf16[32,1024]{1,0:T(8,128)(2,1)S(1)}, u32[]{:S(2)}, u32[]{:S(2)}) collective-permute-start(bf16[32,1024]{1,0:T(8,128)(2,1)S(1)} %get-tuple-element.228.tie), channel_id=1, source_target_pairs={{0,58},{1,59},{2,60},{3,61},{4,62},{5,63},{6,56},{7,57},{8,2},{9,3... | collective-permute-start | bytes 196616 | tf_op jit(solution)/shard_map/ppermute | solution.py:396
  260.0 6.5 %collective-permute-done.69.refs_2_ = bf16[128,1024]{1,0:T(8,128)(2,1)S(1)} collective-permute-done((bf16[128,1024]{1,0:T(8,128)(2,1)S(1)}, bf16[128,1024]{1,0:T(8,128)(2,1)S(1)}, u32[]{:S(2)}, u32[]{:S(2)}) %collective-permute-start.69) | collective-permute-done | bytes 262176 | tf_op jit(solution)/shard_map/ppermute | solution.py:386
  282.8 4.9 %collective-permute-done.81 = bf16[32,1024]{1,0:T(8,128)(2,1)S(1)} collective-permute-done((bf16[32,1024]{1,0:T(8,128)(2,1)S(1)}, bf16[32,1024]{1,0:T(8,128)(2,1)S(1)}, u32[]{:S(2)}, u32[]{:S(2)}) %collective-permute-start.81) | collective-permute-done | bytes 65568 | tf_op jit(solution)/shard_map/ppermute | solution.py:396
  301.9 4.8 %collective-permute-start.90 = (bf16[32,1024]{1,0:T(8,128)(2,1)S(1)}, bf16[32,1024]{1,0:T(8,128)(2,1)S(1)}, u32[]{:S(2)}, u32[]{:S(2)}) collective-permute-start(bf16[32,1024]{1,0:T(8,128)(2,1)S(1)} %get-tuple-element.238), channel_id=1, source_target_pairs={{0,58},{1,59},{2,60},{3,61},{4,62},{5,63},{6,56},{7,57},{8,2},{9,3... | collective-permute-start | bytes 196616 | tf_op jit(solution)/shard_map/ppermute | solution.py:396
  325.2 5.3 %collective-permute-start.101 = (bf16[32,1024]{1,0:T(8,128)(2,1)S(1)}, bf16[32,1024]{1,0:T(8,128)(2,1)S(1)}, u32[]{:S(2)}, u32[]{:S(2)}) collective-permute-start(bf16[32,1024]{1,0:T(8,128)(2,1)S(1)} %get-tuple-element.243), channel_id=1, source_target_pairs={{0,62},{1,63},{2,56},{3,57},{4,58},{5,59},{6,60},{7,61},{8,6},{9,7... | collective-permute-start | bytes 196616 | tf_op jit(solution)/shard_map/ppermute | solution.py:396
  330.5 5.5 %collective-permute-start.100 = (bf16[32,1024]{1,0:T(8,128)(2,1)S(1)}, bf16[32,1024]{1,0:T(8,128)(2,1)S(1)}, u32[]{:S(2)}, u32[]{:S(2)}) collective-permute-start(bf16[32,1024]{1,0:T(8,128)(2,1)S(1)} %get-tuple-element.243), channel_id=1, source_target_pairs={{0,60},{1,61},{2,62},{3,63},{4,56},{5,57},{6,58},{7,59},{8,4},{9,5... | collective-permute-start | bytes 196616 | tf_op jit(solution)/shard_map/ppermute | solution.py:396
  337.4 4.7 %collective-permute-done.99 = bf16[32,1024]{1,0:T(8,128)(2,1)S(1)} collective-permute-done((bf16[32,1024]{1,0:T(8,128)(2,1)S(1)}, bf16[32,1024]{1,0:T(8,128)(2,1)S(1)}, u32[]{:S(2)}, u32[]{:S(2)}) %collective-permute-start.99) | collective-permute-done | bytes 65568 | tf_op jit(solution)/shard_map/ppermute | solution.py:396
  346.3 5.3 %backward_t3.1 = (f32[128,1024]{1,0:T(8,128)S(1)}, bf16[128,1024]{1,0:T(8,128)(2,1)S(1)}, bf16[256,4096]{1,0:T(8,128)(2,1)S(1)}) custom-call(s32[16]{0:T(128)S(1)} %compare_select_fusion.3.info, bf16[128,1024]{1,0:T(8,128)(2,1)S(1)} %constant_dynamic-update-slice_fusion.12.e_own, ...), custom_call_target="tpu_custom_call", output_to_operand_aliasing={{2}: (6, {})} | custom-call | tf_op jit(solution)/shard_map/backward_t3/pallas_call | solution.py:211
  365.6 4.9 %collective-permute-done.108 = bf16[32,1024]{1,0:T(8,128)(2,1)S(1)} collective-permute-done((bf16[32,1024]{1,0:T(8,128)(2,1)S(1)}, bf16[32,1024]{1,0:T(8,128)(2,1)S(1)}, u32[]{:S(2)}, u32[]{:S(2)}) %collective-permute-start.108) | collective-permute-done | bytes 65568 | tf_op jit(solution)/shard_map/ppermute | solution.py:396
  389.3 6.8 %collective-permute-done.117 = bf16[32,1024]{1,0:T(8,128)(2,1)S(1)} collective-permute-done((bf16[32,1024]{1,0:T(8,128)(2,1)S(1)}, bf16[32,1024]{1,0:T(8,128)(2,1)S(1)}, u32[]{:S(2)}, u32[]{:S(2)}) %collective-permute-start.117) | collective-permute-done | bytes 65568 | tf_op jit(solution)/shard_map/ppermute | solution.py:396
  409.9 5.0 %collective-permute-start.128 = (bf16[32,1024]{1,0:T(8,128)(2,1)S(1)}, bf16[32,1024]{1,0:T(8,128)(2,1)S(1)}, u32[]{:S(2)}, u32[]{:S(2)}) collective-permute-start(bf16[32,1024]{1,0:T(8,128)(2,1)S(1)} %get-tuple-element.258), channel_id=1, source_target_pairs={{0,62},{1,63},{2,56},{3,57},{4,58},{5,59},{6,60},{7,61},{8,6},{9,7... | collective-permute-start | bytes 196616 | tf_op jit(solution)/shard_map/ppermute | solution.py:396
  417.4 6.1 %collective-permute-done.126 = bf16[32,1024]{1,0:T(8,128)(2,1)S(1)} collective-permute-done((bf16[32,1024]{1,0:T(8,128)(2,1)S(1)}, bf16[32,1024]{1,0:T(8,128)(2,1)S(1)}, u32[]{:S(2)}, u32[]{:S(2)}) %collective-permute-start.126) | collective-permute-done | bytes 65568 | tf_op jit(solution)/shard_map/ppermute | solution.py:396
  429.4 7.0 %collective-permute-done.130.refs_6_ = bf16[128,1024]{1,0:T(8,128)(2,1)S(1)} collective-permute-done((bf16[128,1024]{1,0:T(8,128)(2,1)S(1)}, bf16[128,1024]{1,0:T(8,128)(2,1)S(1)}, u32[]{:S(2)}, u32[]{:S(2)}) %collective-permute-start.130) | collective-permute-done | bytes 262176 | tf_op jit(solution)/shard_map/ppermute | solution.py:386
  441.3 7.1 %weight_grads_0.1 = (bf16[512,4096]{1,0:T(8,128)(2,1)}, bf16[4096,512]{1,0:T(8,128)(2,1)}, f32[8,128]{1,0:T(8,128)S(1)}) custom-call(s32[16]{0:T(128)S(1)} %compare_select_fusion.3.info, bf16[128,1024]{1,0:T(8,128)(2,1)S(1)} %hold_rows.1.refs_0_, bf16[128,1024]{1,0:T(8,128)(2,1)S(1)} %collective-permute-done.68.refs_1_, ...), custom_call_target="tpu_custom_call" | custom-call | flops 8589934592 | bytes 8388608 | tf_op jit(solution)/shard_map/weight_grads_0/pallas_call | solution.py:283
  461.3 7.1 %weight_grads_1.1 = (bf16[512,4096]{1,0:T(8,128)(2,1)}, bf16[4096,512]{1,0:T(8,128)(2,1)}) custom-call(s32[16]{0:T(128)S(1)} %compare_select_fusion.3.info, bf16[128,1024]{1,0:T(8,128)(2,1)S(1)} %hold_rows.1.refs_0_, bf16[128,1024]{1,0:T(8,128)(2,1)S(1)} %collective-permute-done.68.refs_1_, ...), custom_call_target="tpu_custom_call", output_to_operand_aliasing={{0}: (13, {}), {1}: (14, {})} | custom-call | flops 8589934592 | bytes 8388608 | tf_op jit(solution)/shard_map/weight_grads_1/pallas_call | solution.py:283
  (391 shorter events, 300.3 us)
Async XLA Ops:
  57.6 27.3 %collective-permute-start.17 = (bf16[32,1024]{1,0:T(8,128)(2,1)S(1)}, bf16[32,1024]{1,0:T(8,128)(2,1)S(1)}, u32[]{:S(2)}, u32[]{:S(2)}) collective-permute-start(bf16[32,1024]{1,0:T(8,128)(2,1)S(1)} %fusion.17.tie), channel_id=1, source_target_pairs={{0,14},{1,15},{2,8},{3,9},{4,10},{5,11},{6,12},{7,13},{8,22},{9,23... | collective-permute-start | bytes 196616 | tf_op jit(solution)/shard_map/ppermute | solution.py:396
  62.5 22.4 %collective-permute-start.16 = (bf16[32,1024]{1,0:T(8,128)(2,1)S(1)}, bf16[32,1024]{1,0:T(8,128)(2,1)S(1)}, u32[]{:S(2)}, u32[]{:S(2)}) collective-permute-start(bf16[32,1024]{1,0:T(8,128)(2,1)S(1)} %fusion.17.tie), channel_id=1, source_target_pairs={{0,12},{1,13},{2,14},{3,15},{4,8},{5,9},{6,10},{7,11},{8,20},{9,21... | collective-permute-start | bytes 196616 | tf_op jit(solution)/shard_map/ppermute | solution.py:396
  66.4 18.6 %collective-permute-start.15 = (bf16[32,1024]{1,0:T(8,128)(2,1)S(1)}, bf16[32,1024]{1,0:T(8,128)(2,1)S(1)}, u32[]{:S(2)}, u32[]{:S(2)}) collective-permute-start(bf16[32,1024]{1,0:T(8,128)(2,1)S(1)} %fusion.17.tie), channel_id=1, source_target_pairs={{0,10},{1,11},{2,12},{3,13},{4,14},{5,15},{6,8},{7,9},{8,18},{9,19... | collective-permute-start | bytes 196616 | tf_op jit(solution)/shard_map/ppermute | solution.py:396
  67.9 17.1 %collective-permute-start.14 = (bf16[32,1024]{1,0:T(8,128)(2,1)S(1)}, bf16[32,1024]{1,0:T(8,128)(2,1)S(1)}, u32[]{:S(2)}, u32[]{:S(2)}) collective-permute-start(bf16[32,1024]{1,0:T(8,128)(2,1)S(1)} %fusion.17.tie), channel_id=1, source_target_pairs={{0,8},{1,9},{2,10},{3,11},{4,12},{5,13},{6,14},{7,15},{8,16},{9,17... | collective-permute-start | bytes 196616 | tf_op jit(solution)/shard_map/ppermute | solution.py:396
  96.4 11.3 %collective-permute-start.26 = (bf16[32,1024]{1,0:T(8,128)(2,1)S(1)}, bf16[32,1024]{1,0:T(8,128)(2,1)S(1)}, u32[]{:S(2)}, u32[]{:S(2)}) collective-permute-start(bf16[32,1024]{1,0:T(8,128)(2,1)S(1)} %fusion.14), channel_id=1, source_target_pairs={{0,14},{1,15},{2,8},{3,9},{4,10},{5,11},{6,12},{7,13},{8,22},{9,23... | collective-permute-start | bytes 196616 | tf_op jit(solution)/shard_map/ppermute | solution.py:396
  230.5 10.0 %collective-permute-start.67 = (bf16[32,1024]{1,0:T(8,128)(2,1)S(1)}, bf16[32,1024]{1,0:T(8,128)(2,1)S(1)}, u32[]{:S(2)}, u32[]{:S(2)}) collective-permute-start(bf16[32,1024]{1,0:T(8,128)(2,1)S(1)} %get-tuple-element.328), channel_id=1, source_target_pairs={{0,6},{1,7},{2,0},{3,1},{4,2},{5,3},{6,4},{7,5},{8,14},{9,15},{10,... | collective-permute-start | bytes 196616 | tf_op jit(solution)/shard_map/ppermute | solution.py:405
  241.1 16.4 %collective-permute-start.71 = (bf16[32,1024]{1,0:T(8,128)(2,1)S(1)}, bf16[32,1024]{1,0:T(8,128)(2,1)S(1)}, u32[]{:S(2)}, u32[]{:S(2)}) collective-permute-start(bf16[32,1024]{1,0:T(8,128)(2,1)S(1)} %get-tuple-element.228.tie), channel_id=1, source_target_pairs={{0,56},{1,57},{2,58},{3,59},{4,60},{5,61},{6,62},{7,63},{8,0},{9,1... | collective-permute-start | bytes 196616 | tf_op jit(solution)/shard_map/ppermute | solution.py:396
  241.3 18.7 %collective-permute-start.74 = (bf16[32,1024]{1,0:T(8,128)(2,1)S(1)}, bf16[32,1024]{1,0:T(8,128)(2,1)S(1)}, u32[]{:S(2)}, u32[]{:S(2)}) collective-permute-start(bf16[32,1024]{1,0:T(8,128)(2,1)S(1)} %get-tuple-element.228.tie), channel_id=1, source_target_pairs={{0,62},{1,63},{2,56},{3,57},{4,58},{5,59},{6,60},{7,61},{8,6},{9,7... | collective-permute-start | bytes 196616 | tf_op jit(solution)/shard_map/ppermute | solution.py:396
  241.4 18.5 %collective-permute-start.73 = (bf16[32,1024]{1,0:T(8,128)(2,1)S(1)}, bf16[32,1024]{1,0:T(8,128)(2,1)S(1)}, u32[]{:S(2)}, u32[]{:S(2)}) collective-permute-start(bf16[32,1024]{1,0:T(8,128)(2,1)S(1)} %get-tuple-element.228.tie), channel_id=1, source_target_pairs={{0,60},{1,61},{2,62},{3,63},{4,56},{5,57},{6,58},{7,59},{8,4},{9,5... | collective-permute-start | bytes 196616 | tf_op jit(solution)/shard_map/ppermute | solution.py:396
  242.3 17.5 %collective-permute-start.72 = (bf16[32,1024]{1,0:T(8,128)(2,1)S(1)}, bf16[32,1024]{1,0:T(8,128)(2,1)S(1)}, u32[]{:S(2)}, u32[]{:S(2)}) collective-permute-start(bf16[32,1024]{1,0:T(8,128)(2,1)S(1)} %get-tuple-element.228.tie), channel_id=1, source_target_pairs={{0,58},{1,59},{2,60},{3,61},{4,62},{5,63},{6,56},{7,57},{8,2},{9,3... | collective-permute-start | bytes 196616 | tf_op jit(solution)/shard_map/ppermute | solution.py:396
  253.8 12.8 %collective-permute-start.69 = (bf16[128,1024]{1,0:T(8,128)(2,1)S(1)}, bf16[128,1024]{1,0:T(8,128)(2,1)S(1)}, u32[]{:S(2)}, u32[]{:S(2)}) collective-permute-start(bf16[128,1024]{1,0:T(8,128)(2,1)S(1)} %hold_rows.1.refs_0_), channel_id=1, source_target_pairs={{0,64},{64,0},{1,65},{65,1},{2,66},{66,2},{3,67},{67,3},{4,68},{68... | collective-permute-start | bytes 786440 | tf_op jit(solution)/shard_map/ppermute | solution.py:386
  277.6 10.2 %collective-permute-start.83 = (bf16[32,1024]{1,0:T(8,128)(2,1)S(1)}, bf16[32,1024]{1,0:T(8,128)(2,1)S(1)}, u32[]{:S(2)}, u32[]{:S(2)}) collective-permute-start(bf16[32,1024]{1,0:T(8,128)(2,1)S(1)} %get-tuple-element.233), channel_id=1, source_target_pairs={{0,62},{1,63},{2,56},{3,57},{4,58},{5,59},{6,60},{7,61},{8,6},{9,7... | collective-permute-start | bytes 196616 | tf_op jit(solution)/shard_map/ppermute | solution.py:396
  277.6 10.1 %collective-permute-start.82 = (bf16[32,1024]{1,0:T(8,128)(2,1)S(1)}, bf16[32,1024]{1,0:T(8,128)(2,1)S(1)}, u32[]{:S(2)}, u32[]{:S(2)}) collective-permute-start(bf16[32,1024]{1,0:T(8,128)(2,1)S(1)} %get-tuple-element.233), channel_id=1, source_target_pairs={{0,60},{1,61},{2,62},{3,63},{4,56},{5,57},{6,58},{7,59},{8,4},{9,5... | collective-permute-start | bytes 196616 | tf_op jit(solution)/shard_map/ppermute | solution.py:396
  324.4 13.0 %collective-permute-start.98 = (bf16[32,1024]{1,0:T(8,128)(2,1)S(1)}, bf16[32,1024]{1,0:T(8,128)(2,1)S(1)}, u32[]{:S(2)}, u32[]{:S(2)}) collective-permute-start(bf16[32,1024]{1,0:T(8,128)(2,1)S(1)} %get-tuple-element.243), channel_id=1, source_target_pairs={{0,56},{1,57},{2,58},{3,59},{4,60},{5,61},{6,62},{7,63},{8,0},{9,1... | collective-permute-start | bytes 196616 | tf_op jit(solution)/shard_map/ppermute | solution.py:396
  325.2 17.0 %collective-permute-start.101 = (bf16[32,1024]{1,0:T(8,128)(2,1)S(1)}, bf16[32,1024]{1,0:T(8,128)(2,1)S(1)}, u32[]{:S(2)}, u32[]{:S(2)}) collective-permute-start(bf16[32,1024]{1,0:T(8,128)(2,1)S(1)} %get-tuple-element.243), channel_id=1, source_target_pairs={{0,62},{1,63},{2,56},{3,57},{4,58},{5,59},{6,60},{7,61},{8,6},{9,7... | collective-permute-start | bytes 196616 | tf_op jit(solution)/shard_map/ppermute | solution.py:396
  330.5 11.7 %collective-permute-start.100 = (bf16[32,1024]{1,0:T(8,128)(2,1)S(1)}, bf16[32,1024]{1,0:T(8,128)(2,1)S(1)}, u32[]{:S(2)}, u32[]{:S(2)}) collective-permute-start(bf16[32,1024]{1,0:T(8,128)(2,1)S(1)} %get-tuple-element.243), channel_id=1, source_target_pairs={{0,60},{1,61},{2,62},{3,63},{4,56},{5,57},{6,58},{7,59},{8,4},{9,5... | collective-permute-start | bytes 196616 | tf_op jit(solution)/shard_map/ppermute | solution.py:396
  360.3 10.2 %collective-permute-start.110 = (bf16[32,1024]{1,0:T(8,128)(2,1)S(1)}, bf16[32,1024]{1,0:T(8,128)(2,1)S(1)}, u32[]{:S(2)}, u32[]{:S(2)}) collective-permute-start(bf16[32,1024]{1,0:T(8,128)(2,1)S(1)} %get-tuple-element.248), channel_id=1, source_target_pairs={{0,62},{1,63},{2,56},{3,57},{4,58},{5,59},{6,60},{7,61},{8,6},{9,7... | collective-permute-start | bytes 196616 | tf_op jit(solution)/shard_map/ppermute | solution.py:396
  360.4 10.1 %collective-permute-start.109 = (bf16[32,1024]{1,0:T(8,128)(2,1)S(1)}, bf16[32,1024]{1,0:T(8,128)(2,1)S(1)}, u32[]{:S(2)}, u32[]{:S(2)}) collective-permute-start(bf16[32,1024]{1,0:T(8,128)(2,1)S(1)} %get-tuple-element.248), channel_id=1, source_target_pairs={{0,60},{1,61},{2,62},{3,63},{4,56},{5,57},{6,58},{7,59},{8,4},{9,5... | collective-permute-start | bytes 196616 | tf_op jit(solution)/shard_map/ppermute | solution.py:396
  360.5 10.0 %collective-permute-start.108 = (bf16[32,1024]{1,0:T(8,128)(2,1)S(1)}, bf16[32,1024]{1,0:T(8,128)(2,1)S(1)}, u32[]{:S(2)}, u32[]{:S(2)}) collective-permute-start(bf16[32,1024]{1,0:T(8,128)(2,1)S(1)} %get-tuple-element.248), channel_id=1, source_target_pairs={{0,58},{1,59},{2,60},{3,61},{4,62},{5,63},{6,56},{7,57},{8,2},{9,3... | collective-permute-start | bytes 196616 | tf_op jit(solution)/shard_map/ppermute | solution.py:396
  386.0 10.2 %collective-permute-start.119 = (bf16[32,1024]{1,0:T(8,128)(2,1)S(1)}, bf16[32,1024]{1,0:T(8,128)(2,1)S(1)}, u32[]{:S(2)}, u32[]{:S(2)}) collective-permute-start(bf16[32,1024]{1,0:T(8,128)(2,1)S(1)} %get-tuple-element.253), channel_id=1, source_target_pairs={{0,62},{1,63},{2,56},{3,57},{4,58},{5,59},{6,60},{7,61},{8,6},{9,7... | collective-permute-start | bytes 196616 | tf_op jit(solution)/shard_map/ppermute | solution.py:396
  409.9 13.6 %collective-permute-start.128 = (bf16[32,1024]{1,0:T(8,128)(2,1)S(1)}, bf16[32,1024]{1,0:T(8,128)(2,1)S(1)}, u32[]{:S(2)}, u32[]{:S(2)}) collective-permute-start(bf16[32,1024]{1,0:T(8,128)(2,1)S(1)} %get-tuple-element.258), channel_id=1, source_target_pairs={{0,62},{1,63},{2,56},{3,57},{4,58},{5,59},{6,60},{7,61},{8,6},{9,7... | collective-permute-start | bytes 196616 | tf_op jit(solution)/shard_map/ppermute | solution.py:396
  429.3 12.0 %collective-permute-start.129 = (bf16[128,1024]{1,0:T(8,128)(2,1)S(1)}, bf16[128,1024]{1,0:T(8,128)(2,1)S(1)}, u32[]{:S(2)}, u32[]{:S(2)}) collective-permute-start(bf16[128,1024]{1,0:T(8,128)(2,1)S(1)} %select_select_fusion.refs_4_), channel_id=1, source_target_pairs={{0,1},{1,0},{2,3},{3,2},{4,5},{5,4},{6,7},{7,6},{8,9},{9,8},{10,11... | collective-permute-start | bytes 786440 | tf_op jit(solution)/shard_map/ppermute | solution.py:383
  437.4 11.0 %collective-permute-start.136 = (bf16[32,1024]{1,0:T(8,128)(2,1)S(1)}, bf16[32,1024]{1,0:T(8,128)(2,1)S(1)}, u32[]{:S(2)}, u32[]{:S(2)}) collective-permute-start(bf16[32,1024]{1,0:T(8,128)(2,1)S(1)} %get-tuple-element.307), channel_id=1, source_target_pairs={{0,6},{1,7},{2,0},{3,1},{4,2},{5,3},{6,4},{7,5},{8,14},{9,15},{10,... | collective-permute-start | bytes 196616 | tf_op jit(solution)/shard_map/ppermute | solution.py:405
  437.5 10.9 %collective-permute-start.135 = (bf16[32,1024]{1,0:T(8,128)(2,1)S(1)}, bf16[32,1024]{1,0:T(8,128)(2,1)S(1)}, u32[]{:S(2)}, u32[]{:S(2)}) collective-permute-start(bf16[32,1024]{1,0:T(8,128)(2,1)S(1)} %get-tuple-element.308), channel_id=1, source_target_pairs={{0,4},{1,5},{2,6},{3,7},{4,0},{5,1},{6,2},{7,3},{8,12},{9,13},{10,... | collective-permute-start | bytes 196616 | tf_op jit(solution)/shard_map/ppermute | solution.py:405
  (122 other events, 626.7 us)

commit v3 on v2

--- a/solution.py
+++ b/solution.py
@@ -220,8 +220,7 @@
     )(info, e_own, e_oth, wi, wo, s, p, *ties)
 
 
-def norm_back_body(t, info, total, q1, q2, q3, g, gain, n_save, r_save, gg_in, *refs):
-    out, gg = refs[-2:]
+def norm_back_body(t, info, total, q1, q2, q3, g, gain, n_save, r_save, gg_in, out, gg):
     chunk, width = out.shape
 
     @pl.when(info[t] > 0)
@@ -236,16 +235,36 @@
         out[...] = (back + g[:chunk, :].astype(F32)).astype(BF16)
 
 
-def norm_back_call(t, info, terms, g, gain, n_save, r_save, gg, ties):
+def norm_back_call(t, info, terms, g, gain, n_save, r_save, gg):
     return pl.pallas_call(
         functools.partial(norm_back_body, t),
         out_shape=(jax.ShapeDtypeStruct(n_save.shape, BF16), VMEM(gg.shape, F32)),
-        in_specs=[IN_SMEM] + [IN_VMEM] * 9 + [ANYWHERE] * len(ties),
+        in_specs=[IN_SMEM] + [IN_VMEM] * 9,
         out_specs=[IN_VMEM] * 2,
         input_output_aliases={9: 1},
         compiler_params=params(4),
         name=f"norm_back_t{t}",
-    )(info, *terms, g, gain, n_save, r_save, gg, *ties)
+    )(info, *terms, g, gain, n_save, r_save, gg)
+
+
+def gain_rows_body(t, info, q_own, q_oth, u_own, u_oth, gain, gg_in, gg):
+    @pl.when(info[t] > 0)
+    def _():
+        own = jnp.sum(q_own[...] * u_own[...].astype(F32), axis=0, keepdims=True)
+        other = jnp.sum(q_oth[...].astype(F32) * u_oth[...].astype(F32), axis=0, keepdims=True)
+        gg[0:1, :] = (own + other) / gain[...]
+
+
+def gain_rows_call(t, info, q_own, q_oth, u_own, u_oth, gain, gg):
+    return pl.pallas_call(
+        functools.partial(gain_rows_body, t),
+        out_shape=VMEM(gg.shape, F32),
+        in_specs=[IN_SMEM] + [IN_VMEM] * 6,
+        out_specs=IN_VMEM,
+        input_output_aliases={6: 0},
+        compiler_params=params(4),
+        name=f"gain_rows_t{t}",
+    )(info, q_own, q_oth, u_own, u_oth, gain, gg)
 
 
 def grads_body(groups, base, ties, info, *refs):
@@ -323,7 +342,7 @@
 
 
 def shares_body(count, info, *refs):
-    kept, sent, total = refs[count], refs[count + 1], refs[count + 2]
+    kept, sent, total = refs[count + 1 :]
     width = kept.shape[1]
     total[...] = total_of(refs[:count])
     core = info[CORE]
@@ -331,17 +350,17 @@
     sent[...] = total[:, pl.ds(pl.multiple_of((1 - core) * width, width), width)]
 
 
-def shares_call(info, pieces):
+def shares_call(info, pieces, after):
     rows, width = pieces[0].shape
     return pl.pallas_call(
         functools.partial(shares_body, len(pieces)),
         out_shape=(jax.ShapeDtypeStruct((rows, width // 2), F32),) * 2,
-        in_specs=[IN_SMEM] + [IN_VMEM] * len(pieces),
+        in_specs=[IN_SMEM] + [IN_VMEM] * len(pieces) + [ANYWHERE],
         out_specs=[IN_VMEM] * 2,
         scratch_shapes=[VMEM((rows, width), F32)],
         compiler_params=params(1),
         name="gain_shares",
-    )(info, *pieces)
+    )(info, *pieces, after)
 
 
 def pair_body(a, b, out):
@@ -458,29 +477,28 @@
         q_own, q_oth, p = backward_call(
             t, info, e_own, e_oth, wi, wo, s, p, us + up if t == stages - 2 else []
         )
-        terms = collect(q_own, q_oth)
-        ties = []
-        if t == 0:
-            es = [es, swap(es)]
-            ep = [ep, swap(ep)]
-            first = grads_call(0, info, us, up, es, ep, wi, wo, z, p, [])
-            *first, done = first
-            ties = [done]
-        block, gg = norm_back_call(t, info, terms, g, gain, n_save, r_save, gg, ties)
         if t > 0:
+            terms = collect(q_own, q_oth)
+            block, gg = norm_back_call(t, info, terms, g, gain, n_save, r_save, gg)
             incoming = spread(block, -1)
+        else:
+            gg = gain_rows_call(t, info, q_own, q_oth, *us, gain, gg)
         if t == stages - 1:
             us = after_call(us, block, "hold_rows")
             us = [us, swap(us)]
             up = trade(us[0])
             up = [up, swap(up)]
 
+    es = [es, swap(es)]
+    ep = after_call(ep, q_oth, "hold_peer")
+    ep = [ep, swap(ep)]
     mine, *theirs = quarters_call(info, gg, ring)
     shares = [mine] + [
         lax.ppermute(block, "mp", [(i, turned(i, d + 1)) for i in range(ways)])
         for d, block in enumerate(theirs)
     ]
-    kept, sent = shares_call(info, shares)
+    *first, done = grads_call(0, info, us, up, es, ep, wi, wo, z, p, [])
+    kept, sent = shares_call(info, shares, done)
     share = pair_call(kept, swap(sent), "gain_cores")
     grad_in, grad_out = grads_call(1, info, us, up, es, ep, wi, wo, z, p, list(first) + [share])
     grad_gain = pair_call(share, trade(share), "gain_replicas")[0:1]

time: 477 us -> 469 us (0.983)
  the two profiles are of different devices: /device:TPU:31 before, /device:TPU:1 now
where the time goes in v3:
time: 469 us; the launch traced here: 460 us
  starting transfers between devices  205 us (44%)
  waiting for transfers between devices  151 us (32%)
  Pallas kernels  60.3 us (13%)
  blocking collectives  31.9 us (7%)
  between operations  7.13 us (2%)
    ppermute x56, starting transfers between devices, spread(): out.append(lax.ppermute(block, ('pipe', 'mp'), pairs))  103 us
    ppermute x56, waiting for transfers between devices, spread(): out.append(lax.ppermute(block, ('pipe', 'mp'), pairs))  68.2 us
    ppermute x42, waiting for transfers between devices, collect(): lax.ppermute(block, 'mp', [(i, turned(i, d)) for i in range(ways)])  52.4 us
    ppermute x34, starting transfers between devices, swap(): return lax.ppermute(block, 'mp', core_pairs)  48.1 us
    ppermute x42, starting transfers between devices, collect(): lax.ppermute(block, 'mp', [(i, turned(i, d)) for i in range(ways)])  45.3 us
    all_gather x2, blocking collectives, gathered(): lax.all_gather(array.reshape(ways, chunk, width), 'mp', axis=0, tiled=False)  31.9 us
    ppermute x34, waiting for transfers between devices, swap(): return lax.ppermute(block, 'mp', core_pairs)  26.8 us
    pallas_call x16, Pallas kernels, forward_call(): pl.pallas_call(functools.partial(forward_body, t, side, last), out_shape=...  18.7 us
  transfers between devices with their start and end apart: 138, of which 78 were waited for; matrix products, arithmetic and copies ran while one was open for 0% of the time, Pallas kernels for 7%

profile of v3, /device:TPU:1, one launch (start us, length us, event | category | flops | bytes accessed | tf_op | source)
XLA Modules:
  0.0 459.9 jit_solution(16484049939153353597)
XLA Ops:
  0.6 15.2 %all_gather.6.parts = bf16[8,8,32,128]{3,2,1,0:T(8,128)(2,1)S(1)} all-gather(bf16[1,8,32,128]{3,2,1,0:T(8,128)(2,1)} %bitcast.13), channel_id=1, replica_groups=mesh['dp'=2,'pipe'=8,'mp'=8] {'mp'}, dimensions={0}, use_global_device_ids=true | all-gather | bytes 589824 | tf_op jit(solution)/shard_map/all_gather | solution.py:437
  17.1 5.8 %load_weights.1 = (bf16[1024,4096]{1,0:T(8,128)(2,1)S(1)}, bf16[4096,1024]{1,0:T(8,128)(2,1)S(1)}, bf16[256,4096]{1,0:T(8,128)(2,1)S(1)}, bf16[256,4096]{1,0:T(8...) custom-call(bf16[128,1024]{1,0:T(8,128)(2,1)} %copy-done, ...), custom_call_target="tpu_custom_call" | custom-call | tf_op jit(solution)/shard_map/load_weights/pallas_call | solution.py:54
  42.1 5.9 %collective-permute-done.8.refs_3_ = bf16[32,1024]{1,0:T(8,128)(2,1)S(1)} collective-permute-done((bf16[32,1024]{1,0:T(8,128)(2,1)S(1)}, bf16[32,1024]{1,0:T(8,128)(2,1)S(1)}, u32[]{:S(2)}, u32[]{:S(2)}) %collective-permute-start.8) | collective-permute-done | bytes 65568 | tf_op jit(solution)/shard_map/ppermute | solution.py:415
  69.7 16.7 %all_gather.7.parts = bf16[8,8,32,128]{3,2,1,0:T(8,128)(2,1)S(1)} all-gather(bf16[1,8,32,128]{3,2,1,0:T(8,128)(2,1)S(1)} %bitcast.12), channel_id=1, replica_groups=mesh['dp'=2,'pipe'=8,'mp'=8] {'mp'}, dimensions={0}, use_global_device_ids=true | all-gather | bytes 589824 | tf_op jit(solution)/shard_map/all_gather | solution.py:437
  101.2 7.9 %collective-permute-start.25 = (bf16[32,1024]{1,0:T(8,128)(2,1)S(1)}, bf16[32,1024]{1,0:T(8,128)(2,1)S(1)}, u32[]{:S(2)}, u32[]{:S(2)}) collective-permute-start(bf16[32,1024]{1,0:T(8,128)(2,1)S(1)} %fusion.14), channel_id=1, source_target_pairs={{0,12},{1,13},{2,14},{3,15},{4,8},{5,9},{6,10},{7,11},{8,20},{9,21... | collective-permute-start | bytes 196616 | tf_op jit(solution)/shard_map/ppermute | solution.py:415
  110.6 5.9 %collective-permute-done.24.refs_1_ = bf16[32,1024]{1,0:T(8,128)(2,1)S(1)} collective-permute-done((bf16[32,1024]{1,0:T(8,128)(2,1)S(1)}, bf16[32,1024]{1,0:T(8,128)(2,1)S(1)}, u32[]{:S(2)}, u32[]{:S(2)}) %collective-permute-start.24) | collective-permute-done | bytes 65568 | tf_op jit(solution)/shard_map/ppermute | solution.py:415
  132.2 4.2 collective-permute-start.33
  160.2 6.4 %collective-permute-start.41 = (bf16[32,1024]{1,0:T(8,128)(2,1)S(1)}, bf16[32,1024]{1,0:T(8,128)(2,1)S(1)}, u32[]{:S(2)}, u32[]{:S(2)}) collective-permute-start(bf16[32,1024]{1,0:T(8,128)(2,1)S(1)} %fusion.8), channel_id=1, source_target_pairs={{0,8},{1,9},{2,10},{3,11},{4,12},{5,13},{6,14},{7,15},{8,16},{9,17... | collective-permute-start | bytes 196616 | tf_op jit(solution)/shard_map/ppermute | solution.py:415
  183.0 4.5 collective-permute-start.53
  191.1 4.2 collective-permute-done.52.refs_2_
  241.0 9.6 %collective-permute-start.71 = (bf16[32,1024]{1,0:T(8,128)(2,1)S(1)}, bf16[32,1024]{1,0:T(8,128)(2,1)S(1)}, u32[]{:S(2)}, u32[]{:S(2)}) collective-permute-start(bf16[32,1024]{1,0:T(8,128)(2,1)S(1)} %get-tuple-element.227.tie), channel_id=1, source_target_pairs={{0,56},{1,57},{2,58},{3,59},{4,60},{5,61},{6,62},{7,63},{8,0},{9,1... | collective-permute-start | bytes 196616 | tf_op jit(solution)/shard_map/ppermute | solution.py:415
  280.8 6.0 %collective-permute-done.81 = bf16[32,1024]{1,0:T(8,128)(2,1)S(1)} collective-permute-done((bf16[32,1024]{1,0:T(8,128)(2,1)S(1)}, bf16[32,1024]{1,0:T(8,128)(2,1)S(1)}, u32[]{:S(2)}, u32[]{:S(2)}) %collective-permute-start.81) | collective-permute-done | bytes 65568 | tf_op jit(solution)/shard_map/ppermute | solution.py:415
  300.8 5.5 %collective-permute-start.89 = (bf16[32,1024]{1,0:T(8,128)(2,1)S(1)}, bf16[32,1024]{1,0:T(8,128)(2,1)S(1)}, u32[]{:S(2)}, u32[]{:S(2)}) collective-permute-start(bf16[32,1024]{1,0:T(8,128)(2,1)S(1)} %get-tuple-element.237), channel_id=1, source_target_pairs={{0,56},{1,57},{2,58},{3,59},{4,60},{5,61},{6,62},{7,63},{8,0},{9,1... | collective-permute-start | bytes 196616 | tf_op jit(solution)/shard_map/ppermute | solution.py:415
  308.9 5.0 %collective-permute-start.91 = (bf16[32,1024]{1,0:T(8,128)(2,1)S(1)}, bf16[32,1024]{1,0:T(8,128)(2,1)S(1)}, u32[]{:S(2)}, u32[]{:S(2)}) collective-permute-start(bf16[32,1024]{1,0:T(8,128)(2,1)S(1)} %get-tuple-element.237), channel_id=1, source_target_pairs={{0,60},{1,61},{2,62},{3,63},{4,56},{5,57},{6,58},{7,59},{8,4},{9,5... | collective-permute-start | bytes 196616 | tf_op jit(solution)/shard_map/ppermute | solution.py:415
  314.5 4.6 %collective-permute-done.90 = bf16[32,1024]{1,0:T(8,128)(2,1)S(1)} collective-permute-done((bf16[32,1024]{1,0:T(8,128)(2,1)S(1)}, bf16[32,1024]{1,0:T(8,128)(2,1)S(1)}, u32[]{:S(2)}, u32[]{:S(2)}) %collective-permute-start.90) | collective-permute-done | bytes 65568 | tf_op jit(solution)/shard_map/ppermute | solution.py:415
  339.2 4.8 %collective-permute-done.99 = bf16[32,1024]{1,0:T(8,128)(2,1)S(1)} collective-permute-done((bf16[32,1024]{1,0:T(8,128)(2,1)S(1)}, bf16[32,1024]{1,0:T(8,128)(2,1)S(1)}, u32[]{:S(2)}, u32[]{:S(2)}) %collective-permute-start.99) | collective-permute-done | bytes 65568 | tf_op jit(solution)/shard_map/ppermute | solution.py:415
  357.4 5.1 %collective-permute-start.107 = (bf16[32,1024]{1,0:T(8,128)(2,1)S(1)}, bf16[32,1024]{1,0:T(8,128)(2,1)S(1)}, u32[]{:S(2)}, u32[]{:S(2)}) collective-permute-start(bf16[32,1024]{1,0:T(8,128)(2,1)S(1)} %get-tuple-element.247), channel_id=1, source_target_pairs={{0,56},{1,57},{2,58},{3,59},{4,60},{5,61},{6,62},{7,63},{8,0},{9,1... | collective-permute-start | bytes 196616 | tf_op jit(solution)/shard_map/ppermute | solution.py:415
  363.8 6.1 %collective-permute-done.108 = bf16[32,1024]{1,0:T(8,128)(2,1)S(1)} collective-permute-done((bf16[32,1024]{1,0:T(8,128)(2,1)S(1)}, bf16[32,1024]{1,0:T(8,128)(2,1)S(1)}, u32[]{:S(2)}, u32[]{:S(2)}) %collective-permute-start.108) | collective-permute-done | bytes 65568 | tf_op jit(solution)/shard_map/ppermute | solution.py:415
  383.0 5.2 %collective-permute-start.116 = (bf16[32,1024]{1,0:T(8,128)(2,1)S(1)}, bf16[32,1024]{1,0:T(8,128)(2,1)S(1)}, u32[]{:S(2)}, u32[]{:S(2)}) collective-permute-start(bf16[32,1024]{1,0:T(8,128)(2,1)S(1)} %get-tuple-element.252), channel_id=1, source_target_pairs={{0,56},{1,57},{2,58},{3,59},{4,60},{5,61},{6,62},{7,63},{8,0},{9,1... | collective-permute-start | bytes 196616 | tf_op jit(solution)/shard_map/ppermute | solution.py:415
  392.4 5.8 %collective-permute-done.117 = bf16[32,1024]{1,0:T(8,128)(2,1)S(1)} collective-permute-done((bf16[32,1024]{1,0:T(8,128)(2,1)S(1)}, bf16[32,1024]{1,0:T(8,128)(2,1)S(1)}, u32[]{:S(2)}, u32[]{:S(2)}) %collective-permute-start.117) | collective-permute-done | bytes 65568 | tf_op jit(solution)/shard_map/ppermute | solution.py:415
  419.4 4.4 collective-permute-done.126
  427.2 5.4 %backward_t0.1 = (f32[128,1024]{1,0:T(8,128)S(1)}, bf16[128,1024]{1,0:T(8,128)(2,1)S(1)}, bf16[256,4096]{1,0:T(8,128)(2,1)S(1)}) custom-call(s32[16]{0:T(128)S(1)} %compare_select_fusion.3.info, bf16[128,1024]{1,0:T(8,128)(2,1)S(1)} %constant_dynamic-update-slice_fusion.24.e_own, ...), custom_call_target="tpu_custom_call", output_to_operand_aliasing={{2}: (6, {})} | custom-call | tf_op jit(solution)/shard_map/backward_t0/pallas_call | solution.py:211
  441.7 7.1 %weight_grads_0.1 = (bf16[512,4096]{1,0:T(8,128)(2,1)}, bf16[4096,512]{1,0:T(8,128)(2,1)}, f32[8,128]{1,0:T(8,128)S(1)}) custom-call(s32[16]{0:T(128)S(1)} %compare_select_fusion.3.info, bf16[128,1024]{1,0:T(8,128)(2,1)S(1)} %hold_rows.1.refs_0_.u_own, bf16[128,1024]{1,0:T(8,128)(2,1)S(1)} %collective-permute-done.68.refs_1_.u_oth, ...), custom_call_target="tpu_custom_call" | custom-call | flops 8589934592 | bytes 8388608 | tf_op jit(solution)/shard_map/weight_grads_0/pallas_call | solution.py:302
  451.9 7.1 %weight_grads_1.1 = (bf16[512,4096]{1,0:T(8,128)(2,1)}, bf16[4096,512]{1,0:T(8,128)(2,1)}) custom-call(s32[16]{0:T(128)S(1)} %compare_select_fusion.3.info, bf16[128,1024]{1,0:T(8,128)(2,1)S(1)} %hold_rows.1.refs_0_.u_own, bf16[128,1024]{1,0:T(8,128)(2,1)S(1)} %collective-permute-done.68.refs_1_.u_oth, ...), custom_call_target="tpu_custom_call", output_to_operand_aliasing={{0}: (13, {}), {1}: (14, {})} | custom-call | flops 8589934592 | bytes 8388608 | tf_op jit(solution)/shard_map/weight_grads_1/pallas_call | solution.py:302
  (382 shorter events, 294.2 us)
Async XLA Ops:
  41.9 9.3 %collective-permute-start.7 = (bf16[32,1024]{1,0:T(8,128)(2,1)S(1)}, bf16[32,1024]{1,0:T(8,128)(2,1)S(1)}, u32[]{:S(2)}, u32[]{:S(2)}) collective-permute-start(bf16[32,1024]{1,0:T(8,128)(2,1)S(1)} %fusion.20), channel_id=1, source_target_pairs={{0,12},{1,13},{2,14},{3,15},{4,8},{5,9},{6,10},{7,11},{8,20},{9,21... | collective-permute-start | bytes 196616 | tf_op jit(solution)/shard_map/ppermute | solution.py:415
  41.9 10.2 %collective-permute-start.6 = (bf16[32,1024]{1,0:T(8,128)(2,1)S(1)}, bf16[32,1024]{1,0:T(8,128)(2,1)S(1)}, u32[]{:S(2)}, u32[]{:S(2)}) collective-permute-start(bf16[32,1024]{1,0:T(8,128)(2,1)S(1)} %fusion.20), channel_id=1, source_target_pairs={{0,10},{1,11},{2,12},{3,13},{4,14},{5,15},{6,8},{7,9},{8,18},{9,19... | collective-permute-start | bytes 196616 | tf_op jit(solution)/shard_map/ppermute | solution.py:415
  42.0 10.1 %collective-permute-start.5 = (bf16[32,1024]{1,0:T(8,128)(2,1)S(1)}, bf16[32,1024]{1,0:T(8,128)(2,1)S(1)}, u32[]{:S(2)}, u32[]{:S(2)}) collective-permute-start(bf16[32,1024]{1,0:T(8,128)(2,1)S(1)} %fusion.20), channel_id=1, source_target_pairs={{0,8},{1,9},{2,10},{3,11},{4,12},{5,13},{6,14},{7,15},{8,16},{9,17... | collective-permute-start | bytes 196616 | tf_op jit(solution)/shard_map/ppermute | solution.py:415
  66.4 20.6 %collective-permute-start.17 = (bf16[32,1024]{1,0:T(8,128)(2,1)S(1)}, bf16[32,1024]{1,0:T(8,128)(2,1)S(1)}, u32[]{:S(2)}, u32[]{:S(2)}) collective-permute-start(bf16[32,1024]{1,0:T(8,128)(2,1)S(1)} %fusion.17.tie), channel_id=1, source_target_pairs={{0,14},{1,15},{2,8},{3,9},{4,10},{5,11},{6,12},{7,13},{8,22},{9,23... | collective-permute-start | bytes 196616 | tf_op jit(solution)/shard_map/ppermute | solution.py:415
  69.6 17.5 %collective-permute-start.16 = (bf16[32,1024]{1,0:T(8,128)(2,1)S(1)}, bf16[32,1024]{1,0:T(8,128)(2,1)S(1)}, u32[]{:S(2)}, u32[]{:S(2)}) collective-permute-start(bf16[32,1024]{1,0:T(8,128)(2,1)S(1)} %fusion.17.tie), channel_id=1, source_target_pairs={{0,12},{1,13},{2,14},{3,15},{4,8},{5,9},{6,10},{7,11},{8,20},{9,21... | collective-permute-start | bytes 196616 | tf_op jit(solution)/shard_map/ppermute | solution.py:415
  69.6 17.5 %collective-permute-start.15 = (bf16[32,1024]{1,0:T(8,128)(2,1)S(1)}, bf16[32,1024]{1,0:T(8,128)(2,1)S(1)}, u32[]{:S(2)}, u32[]{:S(2)}) collective-permute-start(bf16[32,1024]{1,0:T(8,128)(2,1)S(1)} %fusion.17.tie), channel_id=1, source_target_pairs={{0,10},{1,11},{2,12},{3,13},{4,14},{5,15},{6,8},{7,9},{8,18},{9,19... | collective-permute-start | bytes 196616 | tf_op jit(solution)/shard_map/ppermute | solution.py:415
  69.6 17.5 %collective-permute-start.14 = (bf16[32,1024]{1,0:T(8,128)(2,1)S(1)}, bf16[32,1024]{1,0:T(8,128)(2,1)S(1)}, u32[]{:S(2)}, u32[]{:S(2)}) collective-permute-start(bf16[32,1024]{1,0:T(8,128)(2,1)S(1)} %fusion.17.tie), channel_id=1, source_target_pairs={{0,8},{1,9},{2,10},{3,11},{4,12},{5,13},{6,14},{7,15},{8,16},{9,17... | collective-permute-start | bytes 196616 | tf_op jit(solution)/shard_map/ppermute | solution.py:415
  99.0 11.7 %collective-permute-start.26 = (bf16[32,1024]{1,0:T(8,128)(2,1)S(1)}, bf16[32,1024]{1,0:T(8,128)(2,1)S(1)}, u32[]{:S(2)}, u32[]{:S(2)}) collective-permute-start(bf16[32,1024]{1,0:T(8,128)(2,1)S(1)} %fusion.14), channel_id=1, source_target_pairs={{0,14},{1,15},{2,8},{3,9},{4,10},{5,11},{6,12},{7,13},{8,22},{9,23... | collective-permute-start | bytes 196616 | tf_op jit(solution)/shard_map/ppermute | solution.py:415
  101.2 9.4 %collective-permute-start.25 = (bf16[32,1024]{1,0:T(8,128)(2,1)S(1)}, bf16[32,1024]{1,0:T(8,128)(2,1)S(1)}, u32[]{:S(2)}, u32[]{:S(2)}) collective-permute-start(bf16[32,1024]{1,0:T(8,128)(2,1)S(1)} %fusion.14), channel_id=1, source_target_pairs={{0,12},{1,13},{2,14},{3,15},{4,8},{5,9},{6,10},{7,11},{8,20},{9,21... | collective-permute-start | bytes 196616 | tf_op jit(solution)/shard_map/ppermute | solution.py:415
  132.2 8.9 %collective-permute-start.34 = (bf16[32,1024]{1,0:T(8,128)(2,1)S(1)}, bf16[32,1024]{1,0:T(8,128)(2,1)S(1)}, u32[]{:S(2)}, u32[]{:S(2)}) collective-permute-start(bf16[32,1024]{1,0:T(8,128)(2,1)S(1)} %fusion.11), channel_id=1, source_target_pairs={{0,12},{1,13},{2,14},{3,15},{4,8},{5,9},{6,10},{7,11},{8,20},{9,21... | collective-permute-start | bytes 196616 | tf_op jit(solution)/shard_map/ppermute | solution.py:415
  157.0 9.6 %collective-permute-start.44 = (bf16[32,1024]{1,0:T(8,128)(2,1)S(1)}, bf16[32,1024]{1,0:T(8,128)(2,1)S(1)}, u32[]{:S(2)}, u32[]{:S(2)}) collective-permute-start(bf16[32,1024]{1,0:T(8,128)(2,1)S(1)} %fusion.8), channel_id=1, source_target_pairs={{0,14},{1,15},{2,8},{3,9},{4,10},{5,11},{6,12},{7,13},{8,22},{9,23... | collective-permute-start | bytes 196616 | tf_op jit(solution)/shard_map/ppermute | solution.py:415
  157.6 9.0 %collective-permute-start.43 = (bf16[32,1024]{1,0:T(8,128)(2,1)S(1)}, bf16[32,1024]{1,0:T(8,128)(2,1)S(1)}, u32[]{:S(2)}, u32[]{:S(2)}) collective-permute-start(bf16[32,1024]{1,0:T(8,128)(2,1)S(1)} %fusion.8), channel_id=1, source_target_pairs={{0,12},{1,13},{2,14},{3,15},{4,8},{5,9},{6,10},{7,11},{8,20},{9,21... | collective-permute-start | bytes 196616 | tf_op jit(solution)/shard_map/ppermute | solution.py:415
  241.0 15.5 %collective-permute-start.71 = (bf16[32,1024]{1,0:T(8,128)(2,1)S(1)}, bf16[32,1024]{1,0:T(8,128)(2,1)S(1)}, u32[]{:S(2)}, u32[]{:S(2)}) collective-permute-start(bf16[32,1024]{1,0:T(8,128)(2,1)S(1)} %get-tuple-element.227.tie), channel_id=1, source_target_pairs={{0,56},{1,57},{2,58},{3,59},{4,60},{5,61},{6,62},{7,63},{8,0},{9,1... | collective-permute-start | bytes 196616 | tf_op jit(solution)/shard_map/ppermute | solution.py:415
  252.9 9.0 %collective-permute-start.69 = (bf16[128,1024]{1,0:T(8,128)(2,1)S(1)}, bf16[128,1024]{1,0:T(8,128)(2,1)S(1)}, u32[]{:S(2)}, u32[]{:S(2)}) collective-permute-start(bf16[128,1024]{1,0:T(8,128)(2,1)S(1)} %hold_rows.1.refs_0_.u_own), channel_id=1, source_target_pairs={{0,64},{64,0},{1,65},{65,1},{2,66},{66,2},{3,67},{67,3},{4,68},{68... | collective-permute-start | bytes 786440 | tf_op jit(solution)/shard_map/ppermute | solution.py:405
  300.8 13.7 %collective-permute-start.89 = (bf16[32,1024]{1,0:T(8,128)(2,1)S(1)}, bf16[32,1024]{1,0:T(8,128)(2,1)S(1)}, u32[]{:S(2)}, u32[]{:S(2)}) collective-permute-start(bf16[32,1024]{1,0:T(8,128)(2,1)S(1)} %get-tuple-element.237), channel_id=1, source_target_pairs={{0,56},{1,57},{2,58},{3,59},{4,60},{5,61},{6,62},{7,63},{8,0},{9,1... | collective-permute-start | bytes 196616 | tf_op jit(solution)/shard_map/ppermute | solution.py:415
  306.3 12.9 %collective-permute-start.92 = (bf16[32,1024]{1,0:T(8,128)(2,1)S(1)}, bf16[32,1024]{1,0:T(8,128)(2,1)S(1)}, u32[]{:S(2)}, u32[]{:S(2)}) collective-permute-start(bf16[32,1024]{1,0:T(8,128)(2,1)S(1)} %get-tuple-element.237), channel_id=1, source_target_pairs={{0,62},{1,63},{2,56},{3,57},{4,58},{5,59},{6,60},{7,61},{8,6},{9,7... | collective-permute-start | bytes 196616 | tf_op jit(solution)/shard_map/ppermute | solution.py:415
  308.9 10.2 %collective-permute-start.91 = (bf16[32,1024]{1,0:T(8,128)(2,1)S(1)}, bf16[32,1024]{1,0:T(8,128)(2,1)S(1)}, u32[]{:S(2)}, u32[]{:S(2)}) collective-permute-start(bf16[32,1024]{1,0:T(8,128)(2,1)S(1)} %get-tuple-element.237), channel_id=1, source_target_pairs={{0,60},{1,61},{2,62},{3,63},{4,56},{5,57},{6,58},{7,59},{8,4},{9,5... | collective-permute-start | bytes 196616 | tf_op jit(solution)/shard_map/ppermute | solution.py:415
  383.0 9.5 %collective-permute-start.116 = (bf16[32,1024]{1,0:T(8,128)(2,1)S(1)}, bf16[32,1024]{1,0:T(8,128)(2,1)S(1)}, u32[]{:S(2)}, u32[]{:S(2)}) collective-permute-start(bf16[32,1024]{1,0:T(8,128)(2,1)S(1)} %get-tuple-element.252), channel_id=1, source_target_pairs={{0,56},{1,57},{2,58},{3,59},{4,60},{5,61},{6,62},{7,63},{8,0},{9,1... | collective-permute-start | bytes 196616 | tf_op jit(solution)/shard_map/ppermute | solution.py:415
  388.2 10.1 %collective-permute-start.119 = (bf16[32,1024]{1,0:T(8,128)(2,1)S(1)}, bf16[32,1024]{1,0:T(8,128)(2,1)S(1)}, u32[]{:S(2)}, u32[]{:S(2)}) collective-permute-start(bf16[32,1024]{1,0:T(8,128)(2,1)S(1)} %get-tuple-element.252), channel_id=1, source_target_pairs={{0,62},{1,63},{2,56},{3,57},{4,58},{5,59},{6,60},{7,61},{8,6},{9,7... | collective-permute-start | bytes 196616 | tf_op jit(solution)/shard_map/ppermute | solution.py:415
  414.5 9.4 %collective-permute-start.128 = (bf16[32,1024]{1,0:T(8,128)(2,1)S(1)}, bf16[32,1024]{1,0:T(8,128)(2,1)S(1)}, u32[]{:S(2)}, u32[]{:S(2)}) collective-permute-start(bf16[32,1024]{1,0:T(8,128)(2,1)S(1)} %get-tuple-element.257), channel_id=1, source_target_pairs={{0,62},{1,63},{2,56},{3,57},{4,58},{5,59},{6,60},{7,61},{8,6},{9,7... | collective-permute-start | bytes 196616 | tf_op jit(solution)/shard_map/ppermute | solution.py:415
  426.1 9.5 %collective-permute-start.130 = (bf16[128,1024]{1,0:T(8,128)(2,1)S(1)}, bf16[128,1024]{1,0:T(8,128)(2,1)S(1)}, u32[]{:S(2)}, u32[]{:S(2)}) collective-permute-start(bf16[128,1024]{1,0:T(8,128)(2,1)S(1)} %select_select_fusion.refs_4_), channel_id=1, source_target_pairs={{0,64},{64,0},{1,65},{65,1},{2,66},{66,2},{3,67},{67,3},{4,68},{68... | collective-permute-start | bytes 786440 | tf_op jit(solution)/shard_map/ppermute | solution.py:405
  426.9 14.8 %collective-permute-start.129 = (bf16[128,1024]{1,0:T(8,128)(2,1)S(1)}, bf16[128,1024]{1,0:T(8,128)(2,1)S(1)}, u32[]{:S(2)}, u32[]{:S(2)}) collective-permute-start(bf16[128,1024]{1,0:T(8,128)(2,1)S(1)} %select_select_fusion.refs_4_), channel_id=1, source_target_pairs={{0,1},{1,0},{2,3},{3,2},{4,5},{5,4},{6,7},{7,6},{8,9},{9,8},{10,11... | collective-permute-start | bytes 786440 | tf_op jit(solution)/shard_map/ppermute | solution.py:402
  437.8 11.1 %collective-permute-start.133 = (f32[8,256]{1,0:T(8,128)S(1)}, f32[8,256]{1,0:T(8,128)S(1)}, u32[]{:S(2)}, u32[]{:S(2)}) collective-permute-start(f32[8,256]{1,0:T(8,128)S(1)} %get-tuple-element.267), channel_id=1, source_target_pairs={{0,2},{1,3},{2,4},{3,5},{4,6},{5,7},{6,0},{7,1},{8,10},{9,11},{10,... | collective-permute-start | bytes 24584 | tf_op jit(solution)/shard_map/ppermute | solution.py:497
  438.1 10.7 %collective-permute-start.134 = (f32[8,256]{1,0:T(8,128)S(1)}, f32[8,256]{1,0:T(8,128)S(1)}, u32[]{:S(2)}, u32[]{:S(2)}) collective-permute-start(f32[8,256]{1,0:T(8,128)S(1)} %get-tuple-element.268), channel_id=1, source_target_pairs={{0,4},{1,5},{2,6},{3,7},{4,0},{5,1},{6,2},{7,3},{8,12},{9,13},{10,... | collective-permute-start | bytes 24584 | tf_op jit(solution)/shard_map/ppermute | solution.py:497
  (118 other events, 592.9 us)
